TPU v7x, 256 devices: a whole 4x4x8 slice. The times are simulated.
256 devices in a mesh: row: 8 (over z), col: 32 (over y, x, core).
Axes of the slice: x: 4, y: 4, z: 8, core: 2. Of those that a mesh axis runs over, the one named last changes fastest.
Arguments:
- blocks: bfloat16 [8, 32, 96, 128, 128], P('row', 'col')
- positions: int32 [8, 32, 96], P('row', 'col'), may hold values from 0 to 255, as said below
- counts: int32 [8, 32], P('row', 'col'), may hold values from 24 to 96, as said below
- sketch: bfloat16 [32768, 288], P(('col', 'row')), may hold values from -6 to 6
Outputs:
- basis: float32 [32768, 288], P(('row', 'col'))
- projected: float32 [32768, 288], P(('col', 'row'))
Inputs may be any that keep to these rules, and one draw needn't show every extreme that they name: `positions`: within one device the 96 slots hold distinct places p, each naming block row p // 8 and block column p % 8 of the device's grid. `counts`: slots from a device's count onward are unused.
All inputs are finite; a program needn't handle non-finite values.
Results may differ from a plain program's by a relative error of at most 0.0026.
The roundings to bfloat16 on the way count: a program that leaves them out, or rounds other values in their place, can miss the bound.
Values may be sent and summed in bfloat16 or wider, within the bound.
A program may use at most 128 MiB of HBM per device.

v0:
```python
import jax
import jax.numpy as jnp
from jax import lax
from jax.sharding import PartitionSpec as P

NBR = 32


def local(blocks, positions, counts, sketch):
    width = sketch.shape[1]
    tiles = blocks[0, 0]
    places = positions[0, 0]
    live = counts[0, 0]
    edge = tiles.shape[1]
    slot_total = tiles.shape[0]
    nrows = NBR
    gathered = lax.all_gather(sketch, "row", axis=0, tiled=True)
    ncols = gathered.shape[0] // edge
    brow = places // ncols
    bcol = places % ncols
    used = lax.iota(jnp.int32, slot_total) < live
    row_hot = ((brow[None, :] == lax.iota(jnp.int32, nrows)[:, None]) & used[None, :]).astype(
        jnp.float32
    )
    col_hot = ((bcol[None, :] == lax.iota(jnp.int32, ncols)[:, None]) & used[None, :]).astype(
        jnp.float32
    )

    def forward(operand):
        parts = jnp.take(operand.reshape(ncols, edge, width), bcol, axis=0)
        prod = jnp.einsum("kij,kjw->kiw", tiles, parts, preferred_element_type=jnp.float32)
        summed = jnp.einsum("bk,kiw->biw", row_hot, prod, precision=lax.Precision.HIGHEST)
        return summed.reshape(nrows * edge, width)

    def backward(operand):
        parts = jnp.take(operand.reshape(nrows, edge, width), brow, axis=0)
        prod = jnp.einsum("kji,kjw->kiw", tiles, parts, preferred_element_type=jnp.float32)
        summed = jnp.einsum("ck,kiw->ciw", col_hot, prod, precision=lax.Precision.HIGHEST)
        return summed.reshape(ncols * edge, width)

    first_local = forward(gathered)
    first = lax.psum(first_local, "col").astype(jnp.bfloat16)
    middle = lax.psum(backward(first), "row").astype(jnp.bfloat16)
    power = lax.psum_scatter(forward(middle), "col", scatter_dimension=0, tiled=True)
    order_total = power.shape[0] * lax.axis_size("row") * lax.axis_size("col")
    local_gram = jnp.dot(
        power.T, power, precision=lax.Precision.HIGHEST, preferred_element_type=jnp.float32
    )
    gram = lax.psum(local_gram, ("row", "col")) / order_total
    lower = jnp.linalg.cholesky(gram)
    basis = jax.scipy.linalg.solve_triangular(lower, power.T, lower=True).T
    basis_full = lax.all_gather(basis.astype(jnp.bfloat16), "col", axis=0, tiled=True)
    projected = lax.psum_scatter(backward(basis_full), "row", scatter_dimension=0, tiled=True)
    return (basis, projected)


def solution(mesh):
    return jax.shard_map(
        local,
        mesh=mesh,
        in_specs=(
            P("row", "col", None, None, None),
            P("row", "col", None),
            P("row", "col"),
            P(("col", "row"), None),
        ),
        out_specs=(P(("row", "col"), None), P(("col", "row"), None)),
        check_vma=False,
    )
```

profile of v0, /device:TPU:1, one launch (start us, length us, event | category | flops | bytes accessed | tf_op | source)
XLA Modules:
  0.0 952.9 jit_solution(16541614848346455253)
XLA Ops:
  7.2 24.7 %all_gather.6 = bf16[1024,288]{0,1:T(8,128)(2,1)S(1)} all-gather(bf16[128,288]{0,1:T(8,128)(2,1)} %param.11), channel_id=1, replica_groups=mesh['row'=8,'col'=32] {'row'}, dimensions={0}, use_global_device_ids=true | all-gather | bytes 663552 | tf_op jit(solution)/shard_map/all_gather | solution.py:17
  34.3 7.4 gather_fusion
  41.7 10.1 %convolution_bitcast_fusion.3 = f32[96,128,288]{1,2,0:T(8,128)} fusion(bf16[96,128,288]{1,2,0:T(8,128)(2,1)} %gather_fusion, pred[96]{0:T(512)(128)(4,1)S(1)} %get-tuple-element.35, bf16[1,1,96,128,128]{4,3,2,1,0:T(8,128)(2,1)S(1)} %copy-done), kind=kOutput, calls=%fused_computation.17 | convolution fusion | flops 909508608 | bytes 24379488 | tf_op jit(solution)/shard_map/kij,kjw->kiw/dot_general | solution.py:31
  51.8 25.1 %fusion.6 = f32[32,128,288]{1,0,2:T(8,128)S(1)} fusion(f32[96,128,288]{1,2,0:T(8,128)} %convolution_bitcast_fusion.3, s32[96]{0:T(128)S(1)} %get-tuple-element.23, pred[96]{0:T(512)(128)(4,1)S(1)} %get-tuple-element.39), kind=kOutput, calls=%fused_computation.12 | convolution fusion | flops 1358960640 | bytes 18874848 | tf_op jit(solution)/shard_map/bk,kiw->biw/dot_general | solution.py:32
  83.4 148.5 %all-reduce.8 = bf16[4096,288]{0,1:T(8,128)(2,1)} all-reduce(f32[4096,288]{0,1:T(8,128)} %bitcast.140), channel_id=1, replica_groups=mesh['row'=8,'col'=32] {'col'}, use_global_device_ids=true, to_apply=%region_0.2 | all-reduce | flops 1179648 | bytes 7077888 | tf_op jit(solution)/shard_map/psum | solution.py:42
  235.3 8.1 gather_fusion.1
  243.4 10.1 %convolution_bitcast_fusion.2 = f32[96,128,288]{1,2,0:T(8,128)} fusion(bf16[96,128,288]{1,2,0:T(8,128)(2,1)} %gather_fusion.1, pred[96]{0:T(512)(128)(4,1)S(1)} %get-tuple-element.22, bf16[1,1,96,128,128]{4,3,2,1,0:T(8,128)(2,1)S(1)} %copy-done), kind=kOutput, calls=%fused_computation.16 | convolution fusion | flops 909508608 | bytes 24379488 | tf_op jit(solution)/shard_map/kji,kjw->kiw/dot_general | solution.py:37
  253.5 13.6 %fusion.4 = f32[8,128,288]{1,0,2:T(8,128)S(1)} fusion(f32[96,128,288]{1,2,0:T(8,128)} %convolution_bitcast_fusion.2, s32[96]{0:T(128)S(1)} %get-tuple-element.36, pred[96]{0:T(512)(128)(4,1)S(1)} %get-tuple-element.39), kind=kOutput, calls=%fused_computation.10 | convolution fusion | flops 339740160 | bytes 15335904 | tf_op jit(solution)/shard_map/ck,kiw->ciw/dot_general | solution.py:38
  268.4 50.1 %all-reduce.9 = bf16[1024,288]{0,1:T(8,128)(2,1)} all-reduce(f32[1024,288]{0,1:T(8,128)} %bitcast.144), channel_id=1, replica_groups=mesh['row'=8,'col'=32] {'row'}, use_global_device_ids=true, to_apply=%region_1.4 | all-reduce | flops 294912 | bytes 1769472 | tf_op jit(solution)/shard_map/psum | solution.py:43
  320.5 7.4 gather_fusion.2
  327.9 10.1 %convolution_bitcast_fusion.1 = f32[96,128,288]{1,2,0:T(8,128)} fusion(bf16[96,128,288]{1,2,0:T(8,128)(2,1)} %gather_fusion.2, pred[96]{0:T(512)(128)(4,1)S(1)} %get-tuple-element.35, bf16[1,1,96,128,128]{4,3,2,1,0:T(8,128)(2,1)S(1)} %copy-done), kind=kOutput, calls=%fused_computation.15 | convolution fusion | flops 909508608 | bytes 24379488 | tf_op jit(solution)/shard_map/kij,kjw->kiw/dot_general | solution.py:31
  338.0 14.4 %fusion.2 = f32[32,128,288]{1,0,2:T(8,128)S(1)} fusion(f32[96,128,288]{1,2,0:T(8,128)} %convolution_bitcast_fusion.1, s32[96]{0:T(128)S(1)} %get-tuple-element.23, pred[96]{0:T(512)(128)(4,1)S(1)} %get-tuple-element.39), kind=kOutput, calls=%fused_computation.8 | convolution fusion | flops 1358960640 | bytes 18874848 | tf_op jit(solution)/shard_map/bk,kiw->biw/dot_general | solution.py:32
  359.0 99.3 %reduce-scatter.3.cloned.1.call-done = f32[128,288]{0,1:T(8,128)} async-done(((f32[4096,288]{0,1:T(8,128)}), f32[128,288]{0,1:T(8,128)}) %reduce-scatter.3.cloned.1.call-update) | async-done | bytes 147472 | tf_op jit(solution)/shard_map/reduce_scatter | solution.py:44
  460.9 254.7 %all-reduce.7.cloned.1.call-done = f32[288,288]{0,1:T(8,128)} async-done(((f32[288,288]{0,1:T(8,128)}), f32[288,288]{0,1:T(8,128)}) %all-reduce.7.cloned.1.call-update) | async-done | bytes 331792 | tf_op jit(solution)/shard_map/psum | solution.py:49
  721.3 11.7 %cholesky.78 = f32[128,128]{1,0:T(8,128)S(1)} custom-call(f32[128,128]{1,0:T(8,128)S(1)} %cholesky.198), custom_call_target="Cholesky" | custom-call | tf_op jit(solution)/shard_map/jit(cholesky)/cholesky | solution.py:50
  733.9 9.8 %custom-call.23 = f32[1,128,128]{1,2,0:T(8,128)S(1)} custom-call(f32[1,128,128]{2,1,0:T(8,128)S(1)} %get-tuple-element.32), custom_call_target="InvertDiagBlocksLowerTriangular" | custom-call | tf_op jit(solution)/shard_map/jit(cholesky)/cholesky | solution.py:50
  747.2 12.5 %cholesky.164 = f32[128,128]{1,0:T(8,128)S(1)} custom-call(f32[128,128]{1,0:T(8,128)} %cholesky.202), custom_call_target="Cholesky" | custom-call | tf_op jit(solution)/shard_map/jit(cholesky)/cholesky | solution.py:50
  760.5 10.8 %custom-call.24 = f32[1,128,128]{1,2,0:T(8,128)S(1)} custom-call(f32[1,128,128]{2,1,0:T(8,128)} %get-tuple-element.29), custom_call_target="InvertDiagBlocksLowerTriangular" | custom-call | tf_op jit(solution)/shard_map/jit(cholesky)/cholesky | solution.py:50
  790.2 30.1 %custom-call.25 = f32[3,128,128]{1,2,0:T(8,128)} custom-call(f32[3,128,128]{2,1,0:T(8,128)S(1)} %pad_maximum_fusion), custom_call_target="InvertDiagBlocksLowerTriangular" | custom-call | tf_op jit(solution)/shard_map/jit(_solve_triangular)/triangular_solve | solution.py:51
  826.3 49.2 %all-gather.2.cloned.1.call-done = bf16[4096,288]{0,1:T(8,128)(2,1)} async-done(((bf16[128,288]{0,1:T(8,128)(2,1)}), bf16[4096,288]{0,1:T(8,128)(2,1)}) %all-gather.2.cloned.1.call-update) | async-done | bytes 2359312 | tf_op jit(solution)/shard_map/all_gather | solution.py:52
  879.0 8.2 gather_fusion.3
  887.2 10.1 %convolution_bitcast_fusion = f32[96,128,288]{1,2,0:T(8,128)} fusion(bf16[96,128,288]{1,2,0:T(8,128)(2,1)} %gather_fusion.3, pred[96]{0:T(512)(128)(4,1)S(1)} %copy-done.10, bf16[1,1,96,128,128]{4,3,2,1,0:T(8,128)(2,1)S(1)} %copy-done), kind=kOutput, calls=%fused_computation.14 | convolution fusion | flops 909508608 | bytes 24379488 | tf_op jit(solution)/shard_map/kji,kjw->kiw/dot_general | solution.py:37
  897.3 13.6 %fusion = f32[8,128,288]{1,0,2:T(8,128)S(1)} fusion(f32[96,128,288]{1,2,0:T(8,128)} %convolution_bitcast_fusion, s32[96]{0:T(128)S(1)} %copy-done.8, pred[96]{0:T(512)(128)(4,1)S(1)} %copy-done.5), kind=kOutput, calls=%fused_computation.6 | convolution fusion | flops 339740160 | bytes 15335904 | tf_op jit(solution)/shard_map/ck,kiw->ciw/dot_general | solution.py:38
  912.2 33.8 %reduce-scatter.5.cloned.1.call-done = f32[128,288]{0,1:T(8,128)} async-done(((f32[1024,288]{0,1:T(8,128)}), f32[128,288]{0,1:T(8,128)}) %reduce-scatter.5.cloned.1.call-update) | async-done | bytes 147472 | tf_op jit(solution)/shard_map/reduce_scatter | solution.py:53
  (83 shorter events, 69.3 us)
Async XLA Ops:
  7.2 34.5 %copy-start = (bf16[1,1,96,128,128]{4,3,2,1,0:T(8,128)(2,1)S(1)}, bf16[1,1,96,128,128]{4,3,2,1,0:T(8,128)(2,1)}, u32[]{:S(2)}) copy-start(bf16[1,1,96,128,128]{4,3,2,1,0:T(8,128)(2,1)} %param.8) | copy-start | bytes 9437188
  7.2 451.1 %reduce-scatter.3.cloned.1.call-start = ((), (), s32[]{:S(2)}) async-start(), calls=%async_computation.2 | async-start | bytes 4866048 | tf_op jit(solution)/shard_map/reduce_scatter | solution.py:44
  34.2 209.2 %copy-start.9 = (pred[96]{0:T(512)(128)(4,1)}, pred[96]{0:T(512)(128)(4,1)S(1)}, u32[]{:S(2)}) copy-start(pred[96]{0:T(512)(128)(4,1)S(1)} %get-tuple-element.22) | copy-start | bytes 292
  34.2 219.3 %copy-start.7 = (s32[96]{0:T(128)}, s32[96]{0:T(128)S(1)}, u32[]{:S(2)}) copy-start(s32[96]{0:T(128)S(1)} %get-tuple-element.36) | copy-start | bytes 1156
  34.2 303.8 %copy-start.4 = (pred[96]{0:T(512)(128)(4,1)}, pred[96]{0:T(512)(128)(4,1)S(1)}, u32[]{:S(2)}) copy-start(pred[96]{0:T(512)(128)(4,1)S(1)} %get-tuple-element.39) | copy-start | bytes 292
  235.3 8.1 copy-start.6
  358.9 356.6 %all-reduce.7.cloned.1.call-start = ((), (), s32[]{:S(2)}) async-start(), calls=%async_computation.3 | async-start | bytes 884736 | tf_op jit(solution)/shard_map/psum | solution.py:49
  458.3 362.1 %copy-start.2 = (f32[128,288]{0,1:T(8,128)S(1)}, f32[128,288]{0,1:T(8,128)}, u32[]{:S(2)}) copy-start(f32[128,288]{0,1:T(8,128)} %reduce-scatter.3.cloned.1.call-done) | copy-start | bytes 442372
  460.6 414.9 %all-gather.2.cloned.1.call-start = ((), (), s32[]{:S(2)}) async-start(), calls=%async_computation.4 | async-start | bytes 2433024 | tf_op jit(solution)/shard_map/all_gather | solution.py:52
  720.6 0.8 copy-start.3
  781.5 0.8 copy-start.1
  826.3 119.7 %reduce-scatter.5.cloned.1.call-start = ((), (), s32[]{:S(2)}) async-start(), calls=%async_computation.5 | async-start | bytes 1327104 | tf_op jit(solution)/shard_map/reduce_scatter | solution.py:53
  879.0 8.2 copy-start.10
  887.2 10.1 %copy-start.5 = (pred[96]{0:T(512)(128)(4,1)S(1)}, pred[96]{0:T(512)(128)(4,1)}, u32[]{:S(2)}) copy-start(pred[96]{0:T(512)(128)(4,1)} %copy-done.4) | copy-start | bytes 292
  887.2 10.1 %copy-start.8 = (s32[96]{0:T(128)S(1)}, s32[96]{0:T(128)}, u32[]{:S(2)}) copy-start(s32[96]{0:T(128)} %copy-done.7) | copy-start | bytes 1156
Sparse Core Ops, SparseCore 0:
  359.0 99.1 reduce-scatter.2
  464.7 250.8 all-reduce.6
  826.4 49.0 all-gather.1
  912.3 33.5 reduce-scatter.4
where the time goes:
time: 965 us; the launch traced here: 953 us
  waiting for transfers between devices  437 us (45%)
  blocking collectives  223 us (23%)
  matrix products  119 us (12%)
  other arithmetic  87.7 us (9%)
  local copies, waits for them, and re-layouts  68.1 us (7%)
  between operations  16.9 us (2%)
    psum x1, waiting for transfers between devices, local(): gram = lax.psum(local_gram, ('row', 'col')) / order_total  255 us
    psum x1, blocking collectives, local(): first = lax.psum(first_local, 'col').astype(jnp.bfloat16)  148 us
    reduce_scatter x1, waiting for transfers between devices, local(): lax.psum_scatter(forward(middle), 'col', scatter_dimension=0, tiled=True)  99.3 us
    another operation x11, other arithmetic, local(): lower = jnp.linalg.cholesky(gram)  51.1 us
    psum x1, blocking collectives, local(): middle = lax.psum(backward(first), 'row').astype(jnp.bfloat16)  50.1 us
    all_gather x1, waiting for transfers between devices, local(): lax.all_gather(basis.astype(jnp.bfloat16), 'col', axis=0, tiled=True)  49.2 us
    dot_general x2, matrix products, forward(): jnp.einsum('bk,kiw->biw', row_hot, prod, precision=lax.Precision.HIGHEST)  39.5 us
    reduce_scatter x1, waiting for transfers between devices, local(): lax.psum_scatter(backward(basis_full), 'row', scatter_dimension=0, tiled=...  33.8 us
  transfers between devices with their start and end apart: 4, of which 4 were waited for; matrix products, arithmetic and copies ran while one was open for 0% of the time, Pallas kernels for 0%

commit v1 on v0

v1 whole, which is shorter than its diff:
```python
import functools

import jax
import jax.numpy as jnp
from jax import lax
from jax.experimental import pallas as pl
from jax.experimental.pallas import tpu as pltpu
from jax.sharding import PartitionSpec as P

MESH = pl.DeviceIdType.MESH
F32 = jnp.float32
BF16 = jnp.bfloat16
DMA = pltpu.SemaphoreType.DMA
HIGHEST = lax.Precision.HIGHEST

NZ = 8
SIDE = 4
CHUNK = 128
WIDTH = 288
HALF = 144
SUB = 96
NSUB = WIDTH // SUB
SLOTS = 96
PACKED = 64


class Place:
    def __init__(self):
        self.r = lax.axis_index("row")
        self.c = lax.axis_index("col")
        self.y = self.c // 8
        self.x = (self.c // 2) % SIDE
        self.k = self.c % 2

    def x_peer(self, i):
        return (self.r, (self.y * SIDE + (self.x + i) % SIDE) * 2 + self.k)

    def y_peer(self, i):
        return (self.r, (((self.y + i) % SIDE) * SIDE + self.x) * 2 + self.k)

    def sibling(self):
        return (self.r, self.c + 1 - 2 * self.k)

    def z_peer(self, i):
        return ((self.r + i) % NZ, self.c)

    def col_peer(self, i):
        return (self.r, (self.c + i) % 32)


def greet(peers):
    barrier = pltpu.get_barrier_semaphore()
    for peer in peers:
        pl.semaphore_signal(barrier, inc=1, device_id=peer, device_id_type=MESH)
    pl.semaphore_wait(barrier, len(peers))


def send(src, dst, send_sem, recv_sem, peer):
    copy = pltpu.make_async_remote_copy(
        src_ref=src,
        dst_ref=dst,
        send_sem=send_sem,
        recv_sem=recv_sem,
        device_id=peer,
        device_id_type=MESH,
    )
    copy.start()
    return copy


def lanes(chunk):
    return pl.ds(pl.multiple_of(chunk * CHUNK, CHUNK), CHUNK)


def gather_z_piece(me, full, sems, piece, pending):
    rows = pl.ds(piece * SUB, SUB)
    send_sem, recv_sem = sems

    def go(step, way):
        owner = (me.r - way * step + NZ) % NZ
        block = full.at[rows, lanes(owner)]
        n = (0 if way == 1 else 4) + step
        copy = send(block, block, send_sem.at[piece, n], recv_sem.at[piece, n], me.z_peer(way % NZ))
        pending.append(copy)
        return copy

    return go


def gather_z(me, full, sems, before=None):
    pending = []
    goes = [gather_z_piece(me, full, sems, piece, pending) for piece in range(NSUB)]
    held = {}
    for step in range(4):
        for piece in range(NSUB):
            if step > 0:
                for copy in held[piece]:
                    copy.wait_recv()
            elif before is not None:
                before(piece)
            copies = [goes[piece](step, 1)]
            if step < 3:
                copies.append(goes[piece](step, -1))
            held[piece] = copies
    for piece in range(NSUB):
        for copy in held[piece]:
            copy.wait_recv()
    return pending


def scatter_z(me, part, up, down, sems, finish):
    send_sem, recv_sem = sems
    pending = []
    held = {}
    for step in range(4):
        for piece in range(NSUB):
            rows = pl.ds(piece * SUB, SUB)
            copies = []
            target = (me.r + 4 + step) % NZ
            if step == 0:
                src = part.at[target, rows]
            else:
                held[piece][0].wait_recv()
                src = up.at[step - 1, rows]
                src[...] += part[target, rows]
            copies.append(
                send(src, up.at[step, rows], send_sem.at[piece, step], recv_sem.at[piece, step], me.z_peer(NZ - 1))
            )
            if step < 3:
                target = (me.r + 3 - step) % NZ
                if step == 0:
                    src = part.at[target, rows]
                else:
                    held[piece][1].wait_recv()
                    src = down.at[step - 1, rows]
                    src[...] += part[target, rows]
                copies.append(
                    send(
                        src, down.at[step, rows], send_sem.at[piece, 4 + step], recv_sem.at[piece, 4 + step], me.z_peer(1)
                    )
                )
            else:
                copies.append(held[piece][1])
            held[piece] = copies
            pending.extend(copies if step < 3 else copies[:1])

    def before(piece):
        rows = pl.ds(piece * SUB, SUB)
        held[piece][0].wait_recv()
        held[piece][1].wait_recv()
        finish(piece, part[me.r, rows] + up[3, rows] + down[2, rows])

    return before, pending


def scatter_col(me, part, other, summed, inbox, inbox2, totals, sems, compute):
    send_sem, recv_sem = sems
    pending = []
    order = [(me.y + i) % SIDE for i in (1, 2, 3, 0)]
    crossing = []
    for i, y in enumerate(order):
        compute(1 - me.k, y)
        crossing.append(send(part.at[1 - me.k, y], other.at[y], send_sem.at[i], recv_sem.at[i], me.sibling()))
    for y in order:
        compute(me.k, y)
    pending.extend(crossing)
    low, high = pl.ds(0, HALF), pl.ds(HALF, HALF)
    first = []
    for i, y in enumerate(order):
        crossing[i].wait_recv()
        for x in range(SIDE):
            summed[y, x] = (part[me.k, y, x] + other[y, x]).astype(summed.dtype)
        if i < 3:
            n = 4 + i
            first.append(
                send(summed.at[y, :, high], inbox.at[1, i], send_sem.at[n], recv_sem.at[n], me.y_peer(i + 1))
            )
    for i in range(3):
        n = 7 + i
        x = (me.x + i + 1) % SIDE
        first.append(send(summed.at[:, x, low], inbox.at[0, i], send_sem.at[n], recv_sem.at[n], me.x_peer(i + 1)))
    for copy in first:
        copy.wait_recv()
    pending.extend(first)
    second = []
    for i in (1, 2, 3, 0):
        y, x = (me.y + i) % SIDE, (me.x + i) % SIDE
        total = summed[y, me.x, low].astype(F32)
        for j in range(3):
            total += inbox[0, j, y].astype(F32)
        totals[0, y] = total.astype(totals.dtype)
        if i:
            n = 9 + i
            second.append(
                send(totals.at[0, y], inbox2.at[0, i - 1], send_sem.at[n], recv_sem.at[n], me.y_peer(i))
            )
        total = summed[me.y, x, high].astype(F32)
        for j in range(3):
            total += inbox[1, j, x].astype(F32)
        totals[1, x] = total.astype(totals.dtype)
        if i:
            n = 12 + i
            second.append(
                send(totals.at[1, x], inbox2.at[1, i - 1], send_sem.at[n], recv_sem.at[n], me.x_peer(i))
            )
    for copy in second:
        copy.wait_recv()
    pending.extend(second)
    halves = []
    for h, mine in enumerate((me.y, me.x)):
        total = totals[h, mine].astype(F32)
        for j in range(3):
            total += inbox2[h, j].astype(F32)
        halves.append(total)
    return halves, pending


def gather_col(me, full, sems):
    send_sem, recv_sem = sems
    pending = []
    k, y, x = me.k, me.y, me.x
    low, high = pl.ds(0, HALF), pl.ds(HALF, HALF)
    first = []
    for i in (1, 2, 3):
        block = full.at[k, y, x, low]
        first.append(send(block, block, send_sem.at[i - 1], recv_sem.at[i - 1], me.y_peer(i)))
        block = full.at[k, y, x, high]
        first.append(send(block, block, send_sem.at[i + 2], recv_sem.at[i + 2], me.x_peer(i)))
    for copy in first:
        copy.wait_recv()
    pending.extend(first)
    second = []
    for i in (1, 2, 3):
        block = full.at[k, :, x, low]
        second.append(send(block, block, send_sem.at[i + 5], recv_sem.at[i + 5], me.x_peer(i)))
        block = full.at[k, y, :, high]
        second.append(send(block, block, send_sem.at[i + 8], recv_sem.at[i + 8], me.y_peer(i)))
    third = []

    def cross(n, block):
        third.append(send(block, block, send_sem.at[n], recv_sem.at[n], me.sibling()))

    cross(12, full.at[k, :, x, low])
    cross(13, full.at[k, y, :, high])
    for i in (1, 3, 2):
        second[2 * i - 2].wait_recv()
        cross(13 + i, full.at[k, :, (x - i + SIDE) % SIDE, low])
        second[2 * i - 1].wait_recv()
        cross(16 + i, full.at[k, (y - i + SIDE) % SIDE, :, high])
    pending.extend(second)
    for copy in third:
        copy.wait_recv()
    pending.extend(third)
    return pending


def dot(a, b, contract, precision=None):
    return lax.dot_general(a, b, ((contract[:1], contract[1:]), ((), ())), precision=precision, preferred_element_type=F32)


def forward(operand, matrix, part):
    def compute(core, y):
        for half in range(2):
            start = pl.multiple_of((core * 16 + y * 4 + half * 2) * CHUNK, 256)
            out = dot(operand[...], matrix[pl.ds(start, 256), :], (1, 1))
            part[core, y, 2 * half] = out[:, :CHUNK]
            part[core, y, 2 * half + 1] = out[:, CHUNK:]

    return compute


def flatten(full, flat):
    def body(n, carry):
        core, y, x = n // 16, (n // 4) % 4, n % 4
        flat[:, pl.ds(pl.multiple_of(n * CHUNK, CHUNK), CHUNK)] = full[core, y, x]
        return carry

    lax.fori_loop(0, 32, body, 0)


def backward(flat, matrix, part):
    def body(n, carry):
        start = pl.multiple_of(n * 256, 256)
        out = dot(flat[...], matrix[:, pl.ds(start, 256)], (1, 0))
        part[2 * n] = out[:, :CHUNK]
        part[2 * n + 1] = out[:, CHUNK:]
        return carry

    lax.fori_loop(0, 4, body, 0)


def packed_tiles():
    return [(g, t) for g in range(36) for t in range((g * 8 + 7) // CHUNK + 1)]


def sample_kernel(
    blocks_ref, slot_ref, sketch_ref, power_ref, gram_ref, matrix_out,
    tiles, matrix, operand, middle, part, other, sum_f, inbox_f, inbox2_f, totals_f,
    sum_h, inbox_h, inbox2_h, totals_h, full, flat, zpart, up, down, gram, packed, gathered, sums, sums_z,
    ga_s, ga_r, gb_s, gb_r, za_s, za_r, ca_s, ca_r, cb_s, cb_r, fa_s, fa_r, g1_s, g1_r, g2_s, g2_r, g3_s, g3_r, local,
):
    me = Place()
    pending = []
    load = pltpu.make_async_copy(blocks_ref, tiles.at[pl.ds(0, SLOTS)], local.at[0])
    load.start()
    greet([me.col_peer(i) for i in range(1, 32)] + [me.z_peer(i) for i in range(1, NZ)])
    operand[:, lanes(me.r)] = sketch_ref[...].astype(F32).T.astype(BF16)
    tiles[SLOTS] = jnp.zeros((CHUNK, CHUNK), BF16)

    load.wait()

    def build(n, carry):
        start = pl.multiple_of(((n % 2) * 16 + n // 2) * CHUNK, CHUNK)
        for t in range(8):
            matrix[pl.ds(start, CHUNK), t * CHUNK : (t + 1) * CHUNK] = tiles[slot_ref[n * 8 + t]]
        return carry

    pending += gather_z(me, operand, (ga_s, ga_r), lambda piece: None)
    lax.fori_loop(0, 32, build, 0)
    keep = pltpu.make_async_copy(matrix, matrix_out, local.at[1])
    keep.start()

    halves, more = scatter_col(
        me, part, other, sum_f, inbox_f, inbox2_f, totals_f, (ca_s, ca_r), forward(operand, matrix, part)
    )
    for copy in more:
        copy.wait_send()
    full[me.k, me.y, me.x, pl.ds(0, HALF)] = halves[0].astype(BF16)
    full[me.k, me.y, me.x, pl.ds(HALF, HALF)] = halves[1].astype(BF16)
    pending += gather_col(me, full, (fa_s, fa_r))
    flatten(full, flat)
    backward(flat, matrix, zpart)

    def finish(piece, total):
        middle[pl.ds(piece * SUB, SUB), lanes(me.r)] = total.astype(BF16)

    before, more = scatter_z(me, zpart, up, down, (za_s, za_r), finish)
    pending += more
    pending += gather_z(me, middle, (gb_s, gb_r), before)

    halves, more = scatter_col(
        me, part, other, sum_h, inbox_h, inbox2_h, totals_h, (cb_s, cb_r), forward(middle, matrix, part)
    )
    pending += more
    power_ref[pl.ds(0, HALF)] = halves[0]
    power_ref[pl.ds(HALF, HALF)] = halves[1]

    gram[...] = jnp.zeros_like(gram)
    gram[:, 0:WIDTH] = dot(power_ref[...], power_ref[...], (1, 1), HIGHEST)
    for n, (g, t) in enumerate(packed_tiles()):
        packed[n] = gram[g * 8 : g * 8 + 8, t * CHUNK : (t + 1) * CHUNK]
    for n in range(len(packed_tiles()), PACKED):
        packed[n] = jnp.zeros((8, CHUNK), F32)
    copies = []
    for i in range(1, 32):
        copies.append(
            send(packed.at[pl.ds(2 * ((me.c + i) % 32), 2)], gathered.at[me.c], g1_s.at[i], g1_r.at[i], me.col_peer(i))
        )
    for copy in copies:
        copy.wait_recv()
    pending += copies
    gathered[me.c] = packed[pl.ds(2 * me.c, 2)]
    total = gathered[0]
    for i in range(1, 32):
        total += gathered[i]
    sums_z[me.r] = total
    copies = []
    for i in (4, 3, 5, 2, 6, 1, 7):
        copies.append(send(sums_z.at[me.r], sums_z.at[me.r], g2_s.at[i], g2_r.at[i], me.z_peer(i)))
    for copy in copies:
        copy.wait_recv()
    pending += copies
    total = sums_z[0]
    for i in range(1, NZ):
        total += sums_z[i]
    sums[me.c] = total
    copies = []
    for i in range(1, 32):
        copies.append(send(sums.at[me.c], sums.at[me.c], g3_s.at[i], g3_r.at[i], me.col_peer(i)))
    for copy in copies:
        copy.wait_recv()
    pending += copies
    for n in range(32):
        gram_ref[2 * n] = sums[n, 0]
        gram_ref[2 * n + 1] = sums[n, 1]
    for copy in pending:
        copy.wait_send()
    keep.wait()


def basis_kernel(gram_ref, power_ref, basis_ref, low_ref, work):
    work[WIDTH:] = jnp.zeros((384 - WIDTH, 512), F32)
    for n, (g, t) in enumerate(packed_tiles()):
        work[g * 8 : g * 8 + 8, t * CHUNK : (t + 1) * CHUNK] = gram_ref[n] * (1.0 / 32768.0)
    work[0:128, 128:256] = work[128:256, 0:128].T
    work[0:128, 256:384] = work[256:384, 0:128].T
    work[128:256, 256:384] = work[256:384, 128:256].T
    work[0:WIDTH, 384:512] = power_ref[...]
    row = lax.broadcasted_iota(jnp.int32, (32, CHUNK), 0)
    lane = lax.broadcasted_iota(jnp.int32, (32, CHUNK), 1)
    for panel in range(9):
        r0 = panel * 32
        tile, off = r0 // CHUNK, r0 % CHUNK
        left = work[r0 : r0 + 32, tile * CHUNK : (tile + 1) * CHUNK]
        right = (lane == row + off).astype(F32)
        for j in range(32):
            col = left[:, off + j : off + j + 1]
            scale = lax.rsqrt(col[j : j + 1])
            pick = row == j
            factor = jnp.where(row > j, col * scale, 0.0)
            left_row = left[j : j + 1] * scale
            right_row = right[j : j + 1] * scale
            left = jnp.where(pick, left_row, left - factor * left_row)
            right = jnp.where(pick, right_row, right - factor * right_row)
        block = pl.ds(tile * CHUNK, CHUNK)
        upper = dot(right, work[block, :], (1, 0), HIGHEST)
        if panel < 8:
            below = work[r0 + 32 : WIDTH, tile * CHUNK : (tile + 1) * CHUNK]
            lower = dot(below, right, (1, 1), HIGHEST)
            work[r0 + 32 : WIDTH, :] -= dot(lower, upper, (1, 0), HIGHEST)
        solved = upper[:, 384:512]
        low_ref[r0 : r0 + 32] = solved.astype(BF16)
        work[r0 : r0 + 32, 384:512] = solved
    basis_ref[...] = work[0:WIDTH, 384:512].T


def project_kernel(
    low_ref, matrix_in, out_ref, matrix, full, flat, zpart, up, down, fa_s, fa_r, za_s, za_r, local
):
    me = Place()
    load = pltpu.make_async_copy(matrix_in, matrix, local.at[0])
    load.start()
    greet(
        [me.x_peer(i) for i in (1, 2, 3)]
        + [me.y_peer(i) for i in (1, 2, 3)]
        + [me.sibling(), me.z_peer(1), me.z_peer(NZ - 1)]
    )
    full[me.k, me.y, me.x] = low_ref[...]
    pending = gather_col(me, full, (fa_s, fa_r))
    flatten(full, flat)
    load.wait()
    backward(flat, matrix, zpart)

    def finish(piece, total):
        out_ref[:, piece * SUB : (piece + 1) * SUB] = total.T

    before, more = scatter_z(me, zpart, up, down, (za_s, za_r), finish)
    for piece in range(NSUB):
        before(piece)
    for copy in pending + more:
        copy.wait_send()


def sem(*shape):
    return [DMA(shape), DMA(shape)]


def local(blocks, positions, counts, sketch):
    places = positions[0, 0]
    used = lax.iota(jnp.int32, SLOTS) < counts[0, 0]
    where = jnp.where(used, places, -1)
    hit = where[None, :] == lax.iota(jnp.int32, 256)[:, None]
    slots = jnp.min(jnp.where(hit, lax.iota(jnp.int32, SLOTS)[None, :], SLOTS), axis=1)

    vmem = pl.BlockSpec(memory_space=pltpu.VMEM)
    hbm = pl.BlockSpec(memory_space=pl.ANY)
    smem = pl.BlockSpec(memory_space=pltpu.SMEM)
    V = pltpu.VMEM
    power, gram, matrix = pl.pallas_call(
        sample_kernel,
        out_shape=[
            jax.ShapeDtypeStruct((WIDTH, CHUNK), F32),
            jax.ShapeDtypeStruct((PACKED, 8, CHUNK), F32),
            jax.ShapeDtypeStruct((4096, 1024), BF16),
        ],
        in_specs=[hbm, smem, vmem],
        out_specs=[vmem, vmem, hbm],
        scratch_shapes=[
            V((SLOTS + 1, CHUNK, CHUNK), BF16),
            V((4096, 1024), BF16),
            V((WIDTH, 1024), BF16),
            V((WIDTH, 1024), BF16),
            V((2, SIDE, SIDE, WIDTH, CHUNK), F32),
            V((SIDE, SIDE, WIDTH, CHUNK), F32),
            V((SIDE, SIDE, WIDTH, CHUNK), F32),
            V((2, 3, SIDE, HALF, CHUNK), F32),
            V((2, 3, HALF, CHUNK), F32),
            V((2, SIDE, HALF, CHUNK), F32),
            V((SIDE, SIDE, WIDTH, CHUNK), BF16),
            V((2, 3, SIDE, HALF, CHUNK), BF16),
            V((2, 3, HALF, CHUNK), BF16),
            V((2, SIDE, HALF, CHUNK), BF16),
            V((2, SIDE, SIDE, WIDTH, CHUNK), BF16),
            V((WIDTH, 4096), BF16),
            V((NZ, WIDTH, CHUNK), F32),
            V((4, WIDTH, CHUNK), F32),
            V((3, WIDTH, CHUNK), F32),
            V((WIDTH, 384), F32),
            V((PACKED, 8, CHUNK), F32),
            V((32, 2, 8, CHUNK), F32),
            V((32, 2, 8, CHUNK), F32),
            V((NZ, 2, 8, CHUNK), F32),
            *sem(NSUB, 7),
            *sem(NSUB, 7),
            *sem(NSUB, 7),
            *sem(16),
            *sem(16),
            *sem(20),
            *sem(32),
            *sem(8),
            *sem(32),
            DMA((2,)),
        ],
        compiler_params=pltpu.CompilerParams(
            collective_id=1, has_side_effects=True, vmem_limit_bytes=56 << 20
        ),
    )(blocks[0, 0], slots, sketch)

    basis, low = pl.pallas_call(
        basis_kernel,
        out_shape=[jax.ShapeDtypeStruct((CHUNK, WIDTH), F32), jax.ShapeDtypeStruct((WIDTH, CHUNK), BF16)],
        in_specs=[vmem, vmem],
        out_specs=[vmem, vmem],
        scratch_shapes=[V((384, 512), F32)],
        compiler_params=pltpu.CompilerParams(vmem_limit_bytes=40 << 20),
    )(gram, power)

    projected = pl.pallas_call(
        project_kernel,
        out_shape=jax.ShapeDtypeStruct((CHUNK, WIDTH), F32),
        in_specs=[vmem, hbm],
        out_specs=vmem,
        scratch_shapes=[
            V((4096, 1024), BF16),
            V((2, SIDE, SIDE, WIDTH, CHUNK), BF16),
            V((WIDTH, 4096), BF16),
            V((NZ, WIDTH, CHUNK), F32),
            V((4, WIDTH, CHUNK), F32),
            V((3, WIDTH, CHUNK), F32),
            *sem(20),
            *sem(NSUB, 7),
            DMA((1,)),
        ],
        compiler_params=pltpu.CompilerParams(
            collective_id=2, has_side_effects=True, vmem_limit_bytes=56 << 20
        ),
    )(low, matrix)
    return (basis, projected)


def solution(mesh):
    return jax.shard_map(
        local,
        mesh=mesh,
        in_specs=(
            P("row", "col", None, None, None),
            P("row", "col", None),
            P("row", "col"),
            P(("col", "row"), None),
        ),
        out_specs=(P(("row", "col"), None), P(("col", "row"), None)),
        check_vma=False,
    )
```

time: 965 us -> 215 us (0.22); the launches traced: 953 us -> 215 us
  waiting for transfers between devices: 437 us -> 0 us
  blocking collectives: 223 us -> 0 us
  Pallas kernels: 0 us -> 206 us
  matrix products: 119 us -> 0 us
  other arithmetic: 87.7 us -> 1.32 us
  local copies, waits for them, and re-layouts: 68.1 us -> 6.58 us
  between operations: 16.9 us -> 1.32 us
    psum x1 -> x0, waiting for transfers between devices: 255 us -> none  [local(): gram = lax.psum(local_gram, ('row', 'col')) / order_total]
    pallas_call x0 -> x3, Pallas kernels: none -> 206 us  [the longest x1 141 us: local(): pl.pallas_call(sample_kernel, out_shape=[jax.ShapeDtypeStruct((WIDTH, CHU...]
    psum x2 -> x0, blocking collectives: 199 us -> none  [the longest x1 148 us: local(): first = lax.psum(first_local, 'col').astype(jnp.bfloat16)]
    reduce_scatter x2 -> x0, waiting for transfers between devices: 133 us -> none  [the longest x1 99.3 us: local(): lax.psum_scatter(forward(middle), 'col', scatter_dimension=0, tiled=True)]
    dot_general x9 -> x0, matrix products: 110 us -> none  [the longest x2 39.5 us: forward(): jnp.einsum('bk,kiw->biw', row_hot, prod, precision=lax.Precision.HIGHEST)]
    another operation x18 -> x0, other arithmetic: 83.3 us -> none  [the longest x11 51.1 us: local(): lower = jnp.linalg.cholesky(gram)]
    all_gather x1 -> x0, waiting for transfers between devices: 49.2 us -> none  [local(): lax.all_gather(basis.astype(jnp.bfloat16), 'col', axis=0, tiled=True)]
    gather x4 -> x0, local copies, waits for them, and re-layouts: 31 us -> none  [the longest x2 16.2 us: backward(): parts = jnp.take(operand.reshape(nrows, edge, width), brow, axis=0)]
  transfers between devices with their start and end apart: 4 -> 0, of which waited for: 4 -> 0; matrix products, arithmetic and copies ran while one was open for 0% -> 0% of each run, Pallas kernels for 0% -> 0%
where the time goes in v1:
time: 215 us
  Pallas kernels  206 us (96%)
  local copies, waits for them, and re-layouts  6.58 us (3%)
    pallas_call x1, Pallas kernels, local(): pl.pallas_call(sample_kernel, out_shape=[jax.ShapeDtypeStruct((WIDTH, CHU...  141 us
    pallas_call x1, Pallas kernels, local(): pl.pallas_call(project_kernel, out_shape=jax.ShapeDtypeStruct((CHUNK, WID...  35.7 us
    pallas_call x1, Pallas kernels, local(): pl.pallas_call(basis_kernel, out_shape=[jax.ShapeDtypeStruct((CHUNK, WIDT...  29 us
    unnamed x9, local copies, waits for them, and re-layouts  6.58 us

profile of v1, /device:TPU:1, one launch (start us, length us, event | category | flops | bytes accessed | tf_op | source)
XLA Modules:
  0.0 215.2 jit_solution(15032917116487372038)
XLA Ops:
  1.3 0.7 compare_select_fusion
  1.9 0.7 select_reduce_fusion.slot_ref
  2.6 1.6 copy.9.sketch_ref
  4.2 141.2 %shard_map.59 = (f32[288,128]{1,0:T(8,128)}, f32[64,8,128]{2,1,0:T(8,128)}, bf16[4096,1024]{1,0:T(8,128)(2,1)}) custom-call(bf16[96,128,128]{2,1,0:T(8,128)(2,1)} %bitcast.5, s32[256]{0:T(256)} %select_reduce_fusion.slot_ref, bf16[128,288]{1,0:T(8,128)(2,1)} %copy.9.sketch_ref), custom_call_target="tpu_custom_call" | custom-call | tf_op jit(solution)/shard_map/pallas_call | solution.py:469
  145.5 0.0 copy-start
  145.5 0.9 copy-done
  146.4 0.0 copy-start.1
  146.4 0.9 copy-done.1
  147.3 29.0 %shard_map.60 = (f32[128,288]{1,0:T(8,128)S(1)}, bf16[288,128]{1,0:T(8,128)(2,1)S(1)}) custom-call(f32[64,8,128]{2,1,0:T(8,128)S(1)} %copy-done, f32[288,128]{1,0:T(8,128)S(1)} %copy-done.1), custom_call_target="tpu_custom_call" | custom-call | tf_op jit(solution)/shard_map/pallas_call | solution.py:519
  176.4 0.0 copy-start.2
  176.4 0.6 copy-done.2
  177.0 35.7 %shard_map.61 = f32[128,288]{1,0:T(8,128)} custom-call(bf16[288,128]{1,0:T(8,128)(2,1)} %copy-done.2, bf16[4096,1024]{1,0:T(8,128)(2,1)} %get-tuple-element.11.matrix_in), custom_call_target="tpu_custom_call" | custom-call | tf_op jit(solution)/shard_map/pallas_call | solution.py:528
  212.7 1.7 copy.11
  214.4 0.8 copy.10
Async XLA Ops:
  145.5 1.0 copy-start
  146.4 0.9 copy-start.1
  176.4 0.6 copy-start.2

commit v2 on v1

--- a/solution.py
+++ b/solution.py
@@ -87,7 +87,7 @@
     return go
 
 
-def gather_z(me, full, sems, before=None):
+def gather_z(me, full, sems, before, meanwhile=None):
     pending = []
     goes = [gather_z_piece(me, full, sems, piece, pending) for piece in range(NSUB)]
     held = {}
@@ -96,12 +96,14 @@
             if step > 0:
                 for copy in held[piece]:
                     copy.wait_recv()
-            elif before is not None:
+            else:
                 before(piece)
             copies = [goes[piece](step, 1)]
             if step < 3:
                 copies.append(goes[piece](step, -1))
             held[piece] = copies
+        if step == 0 and meanwhile is not None:
+            meanwhile()
     for piece in range(NSUB):
         for copy in held[piece]:
             copy.wait_recv()
@@ -215,7 +217,7 @@
     return halves, pending
 
 
-def gather_col(me, full, sems):
+def gather_col(me, full, sems, between=(lambda: None, lambda: None, lambda: None)):
     send_sem, recv_sem = sems
     pending = []
     k, y, x = me.k, me.y, me.x
@@ -226,6 +228,7 @@
         first.append(send(block, block, send_sem.at[i - 1], recv_sem.at[i - 1], me.y_peer(i)))
         block = full.at[k, y, x, high]
         first.append(send(block, block, send_sem.at[i + 2], recv_sem.at[i + 2], me.x_peer(i)))
+    between[0]()
     for copy in first:
         copy.wait_recv()
     pending.extend(first)
@@ -242,12 +245,14 @@
 
     cross(12, full.at[k, :, x, low])
     cross(13, full.at[k, y, :, high])
+    between[1]()
     for i in (1, 3, 2):
         second[2 * i - 2].wait_recv()
         cross(13 + i, full.at[k, :, (x - i + SIDE) % SIDE, low])
         second[2 * i - 1].wait_recv()
         cross(16 + i, full.at[k, (y - i + SIDE) % SIDE, :, high])
     pending.extend(second)
+    between[2]()
     for copy in third:
         copy.wait_recv()
     pending.extend(third)
@@ -294,20 +299,19 @@
 
 
 def sample_kernel(
-    blocks_ref, slot_ref, sketch_ref, power_ref, gram_ref, matrix_out,
+    blocks_ref, slot_ref, sketch_ref, power_ref, second_ref, gram_ref,
     tiles, matrix, operand, middle, part, other, sum_f, inbox_f, inbox2_f, totals_f,
-    sum_h, inbox_h, inbox2_h, totals_h, full, flat, zpart, up, down, gram, packed, gathered, sums, sums_z,
-    ga_s, ga_r, gb_s, gb_r, za_s, za_r, ca_s, ca_r, cb_s, cb_r, fa_s, fa_r, g1_s, g1_r, g2_s, g2_r, g3_s, g3_r, local,
+    sum_h, inbox_h, inbox2_h, totals_h, full, full2, flat, zpart, up, down, up2, down2, gram, packed, gathered, sums, sums_z,
+    ga_s, ga_r, gb_s, gb_r, za_s, za_r, zb_s, zb_r, ca_s, ca_r, cb_s, cb_r, fa_s, fa_r, fb_s, fb_r,
+    g1_s, g1_r, g2_s, g2_r, g3_s, g3_r, local,
 ):
     me = Place()
     pending = []
     load = pltpu.make_async_copy(blocks_ref, tiles.at[pl.ds(0, SLOTS)], local.at[0])
     load.start()
+    operand[:, lanes(me.r)] = sketch_ref[...]
+    tiles[SLOTS] = jnp.zeros((CHUNK, CHUNK), BF16)
     greet([me.col_peer(i) for i in range(1, 32)] + [me.z_peer(i) for i in range(1, NZ)])
-    operand[:, lanes(me.r)] = sketch_ref[...].astype(F32).T.astype(BF16)
-    tiles[SLOTS] = jnp.zeros((CHUNK, CHUNK), BF16)
-
-    load.wait()
 
     def build(n, carry):
         start = pl.multiple_of(((n % 2) * 16 + n // 2) * CHUNK, CHUNK)
@@ -315,10 +319,11 @@
             matrix[pl.ds(start, CHUNK), t * CHUNK : (t + 1) * CHUNK] = tiles[slot_ref[n * 8 + t]]
         return carry
 
-    pending += gather_z(me, operand, (ga_s, ga_r), lambda piece: None)
-    lax.fori_loop(0, 32, build, 0)
-    keep = pltpu.make_async_copy(matrix, matrix_out, local.at[1])
-    keep.start()
+    def build_all():
+        load.wait()
+        lax.fori_loop(0, 32, build, 0)
+
+    pending += gather_z(me, operand, (ga_s, ga_r), lambda piece: None, build_all)
 
     halves, more = scatter_col(
         me, part, other, sum_f, inbox_f, inbox2_f, totals_f, (ca_s, ca_r), forward(operand, matrix, part)
@@ -335,8 +340,9 @@
         middle[pl.ds(piece * SUB, SUB), lanes(me.r)] = total.astype(BF16)
 
     before, more = scatter_z(me, zpart, up, down, (za_s, za_r), finish)
-    pending += more
     pending += gather_z(me, middle, (gb_s, gb_r), before)
+    for copy in more:
+        copy.wait_send()
 
     halves, more = scatter_col(
         me, part, other, sum_h, inbox_h, inbox2_h, totals_h, (cb_s, cb_r), forward(middle, matrix, part)
@@ -344,111 +350,134 @@
     pending += more
     power_ref[pl.ds(0, HALF)] = halves[0]
     power_ref[pl.ds(HALF, HALF)] = halves[1]
-
-    gram[...] = jnp.zeros_like(gram)
-    gram[:, 0:WIDTH] = dot(power_ref[...], power_ref[...], (1, 1), HIGHEST)
-    for n, (g, t) in enumerate(packed_tiles()):
-        packed[n] = gram[g * 8 : g * 8 + 8, t * CHUNK : (t + 1) * CHUNK]
-    for n in range(len(packed_tiles()), PACKED):
-        packed[n] = jnp.zeros((8, CHUNK), F32)
-    copies = []
-    for i in range(1, 32):
-        copies.append(
-            send(packed.at[pl.ds(2 * ((me.c + i) % 32), 2)], gathered.at[me.c], g1_s.at[i], g1_r.at[i], me.col_peer(i))
-        )
-    for copy in copies:
+    full2[me.k, me.y, me.x, pl.ds(0, HALF)] = halves[0].astype(BF16)
+    full2[me.k, me.y, me.x, pl.ds(HALF, HALF)] = halves[1].astype(BF16)
+
+    sent = []
+
+    def gram_part():
+        gram[...] = jnp.zeros_like(gram)
+        gram[:, 0:WIDTH] = dot(power_ref[...], power_ref[...], (1, 1), HIGHEST)
+        for n, (g, t) in enumerate(packed_tiles()):
+            packed[n] = gram[g * 8 : g * 8 + 8, t * CHUNK : (t + 1) * CHUNK]
+        for n in range(len(packed_tiles()), PACKED):
+            packed[n] = jnp.zeros((8, CHUNK), F32)
+        for i in range(1, 32):
+            sent.append(
+                send(packed.at[pl.ds(2 * ((me.c + i) % 32), 2)], gathered.at[me.c], g1_s.at[i], g1_r.at[i], me.col_peer(i))
+            )
+
+    def gram_col():
+        for copy in sent:
+            copy.wait_recv()
+        gathered[me.c] = packed[pl.ds(2 * me.c, 2)]
+        total = gathered[0]
+        for i in range(1, 32):
+            total += gathered[i]
+        sums_z[me.r] = total
+        pending.extend(sent)
+        sent.clear()
+        for i in (4, 3, 5, 2, 6, 1, 7):
+            sent.append(send(sums_z.at[me.r], sums_z.at[me.r], g2_s.at[i], g2_r.at[i], me.z_peer(i)))
+
+    def gram_row():
+        for copy in sent:
+            copy.wait_recv()
+        total = sums_z[0]
+        for i in range(1, NZ):
+            total += sums_z[i]
+        sums[me.c] = total
+        pending.extend(sent)
+        sent.clear()
+        for i in range(1, 32):
+            sent.append(send(sums.at[me.c], sums.at[me.c], g3_s.at[i], g3_r.at[i], me.col_peer(i)))
+
+    pending += gather_col(me, full2, (fb_s, fb_r), (gram_part, gram_col, gram_row))
+    pending.extend(sent)
+    flatten(full2, flat)
+    backward(flat, matrix, zpart)
+
+    def keep(piece, total):
+        second_ref[piece * SUB : (piece + 1) * SUB] = total
+
+    before, more = scatter_z(me, zpart, up2, down2, (zb_s, zb_r), keep)
+    pending += more
+    for copy in sent:
         copy.wait_recv()
-    pending += copies
-    gathered[me.c] = packed[pl.ds(2 * me.c, 2)]
-    total = gathered[0]
-    for i in range(1, 32):
-        total += gathered[i]
-    sums_z[me.r] = total
-    copies = []
-    for i in (4, 3, 5, 2, 6, 1, 7):
-        copies.append(send(sums_z.at[me.r], sums_z.at[me.r], g2_s.at[i], g2_r.at[i], me.z_peer(i)))
-    for copy in copies:
-        copy.wait_recv()
-    pending += copies
-    total = sums_z[0]
-    for i in range(1, NZ):
-        total += sums_z[i]
-    sums[me.c] = total
-    copies = []
-    for i in range(1, 32):
-        copies.append(send(sums.at[me.c], sums.at[me.c], g3_s.at[i], g3_r.at[i], me.col_peer(i)))
-    for copy in copies:
-        copy.wait_recv()
-    pending += copies
     for n in range(32):
         gram_ref[2 * n] = sums[n, 0]
         gram_ref[2 * n + 1] = sums[n, 1]
+    for piece in range(NSUB):
+        before(piece)
     for copy in pending:
         copy.wait_send()
-    keep.wait()
-
-
-def basis_kernel(gram_ref, power_ref, basis_ref, low_ref, work):
-    work[WIDTH:] = jnp.zeros((384 - WIDTH, 512), F32)
+
+
+def over_lanes(block, lane):
+    return jnp.broadcast_to(block[:, lane : lane + 1], (8, CHUNK))
+
+
+def over_rows(block, row):
+    return jnp.broadcast_to(block[row : row + 1, :], (8, CHUNK))
+
+
+def invert_factor(left, off):
+    row = lax.broadcasted_iota(jnp.int32, (8, CHUNK), 0)
+    lane = lax.broadcasted_iota(jnp.int32, (8, CHUNK), 1)
+    L = [left[8 * h : 8 * h + 8] for h in range(4)]
+    R = [(lane == row + 8 * h + off).astype(F32) for h in range(4)]
+    for g in range(4):
+        cols = {h: [over_lanes(L[h], off + 8 * g + b) for b in range(8)] for h in range(g, 4)}
+        p = [[over_rows(cols[g][b], a) for b in range(a + 1)] for a in range(8)]
+        left_rows = [over_rows(L[g], a) for a in range(8)]
+        right_rows = [over_rows(R[g], a) for a in range(8)]
+        for b in range(8):
+            inv = lax.rsqrt(p[b][b])
+            for a in range(b + 1, 8):
+                p[a][b] = p[a][b] * inv
+            for a in range(b + 1, 8):
+                for c in range(b + 1, a + 1):
+                    p[a][c] = p[a][c] - p[a][b] * p[c][b]
+            left_rows[b] = left_rows[b] * inv
+            right_rows[b] = right_rows[b] * inv
+            for a in range(b + 1, 8):
+                left_rows[a] = left_rows[a] - p[a][b] * left_rows[b]
+                right_rows[a] = right_rows[a] - p[a][b] * right_rows[b]
+            for h in range(g + 1, 4):
+                cols[h][b] = cols[h][b] * inv
+                for a in range(b + 1, 8):
+                    cols[h][a] = cols[h][a] - p[a][b] * cols[h][b]
+        for h in range(g + 1, 4):
+            for b in range(8):
+                L[h] = L[h] - cols[h][b] * left_rows[b]
+                R[h] = R[h] - cols[h][b] * right_rows[b]
+        new = right_rows[0]
+        for a in range(1, 8):
+            new = jnp.where(row == a, right_rows[a], new)
+        R[g] = new
+    return jnp.concatenate(R, 0)
+
+
+def basis_kernel(gram_ref, power_ref, second_ref, basis_ref, projected_ref, work):
+    work[WIDTH:] = jnp.zeros((384 - WIDTH, 640), F32)
     for n, (g, t) in enumerate(packed_tiles()):
         work[g * 8 : g * 8 + 8, t * CHUNK : (t + 1) * CHUNK] = gram_ref[n] * (1.0 / 32768.0)
     work[0:128, 128:256] = work[128:256, 0:128].T
     work[0:128, 256:384] = work[256:384, 0:128].T
     work[128:256, 256:384] = work[256:384, 128:256].T
     work[0:WIDTH, 384:512] = power_ref[...]
-    row = lax.broadcasted_iota(jnp.int32, (32, CHUNK), 0)
-    lane = lax.broadcasted_iota(jnp.int32, (32, CHUNK), 1)
+    work[0:WIDTH, 512:640] = second_ref[...]
     for panel in range(9):
         r0 = panel * 32
         tile, off = r0 // CHUNK, r0 % CHUNK
-        left = work[r0 : r0 + 32, tile * CHUNK : (tile + 1) * CHUNK]
-        right = (lane == row + off).astype(F32)
-        for j in range(32):
-            col = left[:, off + j : off + j + 1]
-            scale = lax.rsqrt(col[j : j + 1])
-            pick = row == j
-            factor = jnp.where(row > j, col * scale, 0.0)
-            left_row = left[j : j + 1] * scale
-            right_row = right[j : j + 1] * scale
-            left = jnp.where(pick, left_row, left - factor * left_row)
-            right = jnp.where(pick, right_row, right - factor * right_row)
-        block = pl.ds(tile * CHUNK, CHUNK)
-        upper = dot(right, work[block, :], (1, 0), HIGHEST)
+        right = invert_factor(work[r0 : r0 + 32, tile * CHUNK : (tile + 1) * CHUNK], off)
+        upper = dot(right, work[tile * CHUNK : (tile + 1) * CHUNK, tile * CHUNK :], (1, 0), HIGHEST)
         if panel < 8:
             below = work[r0 + 32 : WIDTH, tile * CHUNK : (tile + 1) * CHUNK]
             lower = dot(below, right, (1, 1), HIGHEST)
-            work[r0 + 32 : WIDTH, :] -= dot(lower, upper, (1, 0), HIGHEST)
-        solved = upper[:, 384:512]
-        low_ref[r0 : r0 + 32] = solved.astype(BF16)
-        work[r0 : r0 + 32, 384:512] = solved
-    basis_ref[...] = work[0:WIDTH, 384:512].T
-
-
-def project_kernel(
-    low_ref, matrix_in, out_ref, matrix, full, flat, zpart, up, down, fa_s, fa_r, za_s, za_r, local
-):
-    me = Place()
-    load = pltpu.make_async_copy(matrix_in, matrix, local.at[0])
-    load.start()
-    greet(
-        [me.x_peer(i) for i in (1, 2, 3)]
-        + [me.y_peer(i) for i in (1, 2, 3)]
-        + [me.sibling(), me.z_peer(1), me.z_peer(NZ - 1)]
-    )
-    full[me.k, me.y, me.x] = low_ref[...]
-    pending = gather_col(me, full, (fa_s, fa_r))
-    flatten(full, flat)
-    load.wait()
-    backward(flat, matrix, zpart)
-
-    def finish(piece, total):
-        out_ref[:, piece * SUB : (piece + 1) * SUB] = total.T
-
-    before, more = scatter_z(me, zpart, up, down, (za_s, za_r), finish)
-    for piece in range(NSUB):
-        before(piece)
-    for copy in pending + more:
-        copy.wait_send()
+            work[r0 + 32 : WIDTH, tile * CHUNK :] -= dot(lower, upper, (1, 0), HIGHEST)
+        basis_ref[r0 : r0 + 32] = upper[:, -256:-128]
+        projected_ref[r0 : r0 + 32] = upper[:, -128:]
 
 
 def sem(*shape):
@@ -466,15 +495,15 @@
     hbm = pl.BlockSpec(memory_space=pl.ANY)
     smem = pl.BlockSpec(memory_space=pltpu.SMEM)
     V = pltpu.VMEM
-    power, gram, matrix = pl.pallas_call(
+    power, second, gram = pl.pallas_call(
         sample_kernel,
         out_shape=[
             jax.ShapeDtypeStruct((WIDTH, CHUNK), F32),
+            jax.ShapeDtypeStruct((WIDTH, CHUNK), F32),
             jax.ShapeDtypeStruct((PACKED, 8, CHUNK), F32),
-            jax.ShapeDtypeStruct((4096, 1024), BF16),
         ],
         in_specs=[hbm, smem, vmem],
-        out_specs=[vmem, vmem, hbm],
+        out_specs=[vmem, vmem, vmem],
         scratch_shapes=[
             V((SLOTS + 1, CHUNK, CHUNK), BF16),
             V((4096, 1024), BF16),
@@ -491,8 +520,11 @@
             V((2, 3, HALF, CHUNK), BF16),
             V((2, SIDE, HALF, CHUNK), BF16),
             V((2, SIDE, SIDE, WIDTH, CHUNK), BF16),
+            V((2, SIDE, SIDE, WIDTH, CHUNK), BF16),
             V((WIDTH, 4096), BF16),
             V((NZ, WIDTH, CHUNK), F32),
+            V((4, WIDTH, CHUNK), F32),
+            V((3, WIDTH, CHUNK), F32),
             V((4, WIDTH, CHUNK), F32),
             V((3, WIDTH, CHUNK), F32),
             V((WIDTH, 384), F32),
@@ -503,49 +535,30 @@
             *sem(NSUB, 7),
             *sem(NSUB, 7),
             *sem(NSUB, 7),
+            *sem(NSUB, 7),
             *sem(16),
             *sem(16),
+            *sem(20),
             *sem(20),
             *sem(32),
             *sem(8),
             *sem(32),
-            DMA((2,)),
+            DMA((1,)),
         ],
         compiler_params=pltpu.CompilerParams(
             collective_id=1, has_side_effects=True, vmem_limit_bytes=56 << 20
         ),
-    )(blocks[0, 0], slots, sketch)
-
-    basis, low = pl.pallas_call(
+    )(blocks[0, 0], slots, sketch.T)
+
+    basis, projected = pl.pallas_call(
         basis_kernel,
-        out_shape=[jax.ShapeDtypeStruct((CHUNK, WIDTH), F32), jax.ShapeDtypeStruct((WIDTH, CHUNK), BF16)],
-        in_specs=[vmem, vmem],
-        out_specs=[vmem, vmem],
-        scratch_shapes=[V((384, 512), F32)],
+        out_shape=[jax.ShapeDtypeStruct((WIDTH, CHUNK), F32)] * 2,
+        in_specs=[vmem] * 3,
+        out_specs=[vmem] * 2,
+        scratch_shapes=[V((384, 640), F32)],
         compiler_params=pltpu.CompilerParams(vmem_limit_bytes=40 << 20),
-    )(gram, power)
-
-    projected = pl.pallas_call(
-        project_kernel,
-        out_shape=jax.ShapeDtypeStruct((CHUNK, WIDTH), F32),
-        in_specs=[vmem, hbm],
-        out_specs=vmem,
-        scratch_shapes=[
-            V((4096, 1024), BF16),
-            V((2, SIDE, SIDE, WIDTH, CHUNK), BF16),
-            V((WIDTH, 4096), BF16),
-            V((NZ, WIDTH, CHUNK), F32),
-            V((4, WIDTH, CHUNK), F32),
-            V((3, WIDTH, CHUNK), F32),
-            *sem(20),
-            *sem(NSUB, 7),
-            DMA((1,)),
-        ],
-        compiler_params=pltpu.CompilerParams(
-            collective_id=2, has_side_effects=True, vmem_limit_bytes=56 << 20
-        ),
-    )(low, matrix)
-    return (basis, projected)
+    )(gram, power, second)
+    return (basis.T, projected.T)
 
 
 def solution(mesh):

time: 215 us -> 174 us (0.81)
  Pallas kernels: 206 us -> 169 us
  local copies, waits for them, and re-layouts: 6.58 us -> 2.76 us
    pallas_call x2 -> x1, Pallas kernels: 64.7 us -> 13.2 us  [local(): pl.pallas_call(basis_kernel, out_shape=[jax.ShapeDtypeStruct((WIDTH, CHUN...]
    pallas_call x1, Pallas kernels: 141 us -> 156 us  [local(): pl.pallas_call(sample_kernel, out_shape=[jax.ShapeDtypeStruct((WIDTH, CHU...]
    unnamed x9 -> x6, local copies, waits for them, and re-layouts: 6.58 us -> 2.76 us
where the time goes in v2:
time: 174 us
  Pallas kernels  169 us (97%)
  local copies, waits for them, and re-layouts  2.76 us (2%)
    pallas_call x1, Pallas kernels, local(): pl.pallas_call(sample_kernel, out_shape=[jax.ShapeDtypeStruct((WIDTH, CHU...  156 us
    pallas_call x1, Pallas kernels, local(): pl.pallas_call(basis_kernel, out_shape=[jax.ShapeDtypeStruct((WIDTH, CHUN...  13.2 us

profile of v2, /device:TPU:1, one launch (start us, length us, event | category | flops | bytes accessed | tf_op | source)
XLA Modules:
  0.0 174.3 jit_solution(18335876910250228107)
XLA Ops:
  1.3 0.7 compare_select_fusion
  1.9 0.7 select_reduce_fusion.slot_ref
  2.6 155.7 %shard_map.59 = (f32[288,128]{1,0:T(8,128)}, f32[288,128]{1,0:T(8,128)}, f32[64,8,128]{2,1,0:T(8,128)}) custom-call(bf16[96,128,128]{2,1,0:T(8,128)(2,1)} %bitcast.8, s32[256]{0:T(256)} %select_reduce_fusion.slot_ref, bf16[288,128]{1,0:T(8,128)(2,1)} %bitcast.9), custom_call_target="tpu_custom_call" | custom-call | tf_op jit(solution)/shard_map/pallas_call | solution.py:498
  158.3 0.0 copy-start
  158.3 0.9 copy-done
  159.2 0.0 copy-start.1
  159.2 0.9 copy-done.1
  160.2 0.0 copy-start.2
  160.2 0.9 copy-done.2
  161.1 13.2 %shard_map.60 = (f32[288,128]{1,0:T(8,128)}, f32[288,128]{1,0:T(8,128)}) custom-call(f32[64,8,128]{2,1,0:T(8,128)S(1)} %copy-done, f32[288,128]{1,0:T(8,128)S(1)} %copy-done.1, f32[288,128]{1,0:T(8,128)S(1)} %copy-done.2), custom_call_target="tpu_custom_call" | custom-call | tf_op jit(solution)/shard_map/pallas_call | solution.py:553
Async XLA Ops:
  158.3 1.0 copy-start
  159.2 0.9 copy-start.1
  160.2 0.9 copy-start.2

commit v3 on v2

--- a/solution.py
+++ b/solution.py
@@ -110,7 +110,7 @@
     return pending
 
 
-def scatter_z(me, part, up, down, sems, finish):
+def scatter_z(me, part, up, down, sems, finish, between=lambda step: None):
     send_sem, recv_sem = sems
     pending = []
     held = {}
@@ -145,6 +145,7 @@
                 copies.append(held[piece][1])
             held[piece] = copies
             pending.extend(copies if step < 3 else copies[:1])
+        between(step)
 
     def before(piece):
         rows = pl.ds(piece * SUB, SUB)
@@ -299,9 +300,10 @@
 
 
 def sample_kernel(
-    blocks_ref, slot_ref, sketch_ref, power_ref, second_ref, gram_ref,
+    blocks_ref, slot_ref, sketch_ref, basis_ref, projected_ref,
     tiles, matrix, operand, middle, part, other, sum_f, inbox_f, inbox2_f, totals_f,
     sum_h, inbox_h, inbox2_h, totals_h, full, full2, flat, zpart, up, down, up2, down2, gram, packed, gathered, sums, sums_z,
+    power, work, right_side,
     ga_s, ga_r, gb_s, gb_r, za_s, za_r, zb_s, zb_r, ca_s, ca_r, cb_s, cb_r, fa_s, fa_r, fb_s, fb_r,
     g1_s, g1_r, g2_s, g2_r, g3_s, g3_r, local,
 ):
@@ -348,8 +350,8 @@
         me, part, other, sum_h, inbox_h, inbox2_h, totals_h, (cb_s, cb_r), forward(middle, matrix, part)
     )
     pending += more
-    power_ref[pl.ds(0, HALF)] = halves[0]
-    power_ref[pl.ds(HALF, HALF)] = halves[1]
+    power[pl.ds(0, HALF)] = halves[0]
+    power[pl.ds(HALF, HALF)] = halves[1]
     full2[me.k, me.y, me.x, pl.ds(0, HALF)] = halves[0].astype(BF16)
     full2[me.k, me.y, me.x, pl.ds(HALF, HALF)] = halves[1].astype(BF16)
 
@@ -357,7 +359,7 @@
 
     def gram_part():
         gram[...] = jnp.zeros_like(gram)
-        gram[:, 0:WIDTH] = dot(power_ref[...], power_ref[...], (1, 1), HIGHEST)
+        gram[:, 0:WIDTH] = dot(power[...], power[...], (1, 1), HIGHEST)
         for n, (g, t) in enumerate(packed_tiles()):
             packed[n] = gram[g * 8 : g * 8 + 8, t * CHUNK : (t + 1) * CHUNK]
         for n in range(len(packed_tiles()), PACKED):
@@ -398,17 +400,26 @@
     backward(flat, matrix, zpart)
 
     def keep(piece, total):
-        second_ref[piece * SUB : (piece + 1) * SUB] = total
-
-    before, more = scatter_z(me, zpart, up2, down2, (zb_s, zb_r), keep)
+        right_side[piece * SUB : (piece + 1) * SUB, CHUNK:] = total
+
+    def between(step):
+        if step == 0:
+            for copy in sent:
+                copy.wait_recv()
+            unpack_gram(sums, work)
+        for panel in (2 * step, 2 * step + 1):
+            eliminate(work, panel)
+
+    before, more = scatter_z(me, zpart, up2, down2, (zb_s, zb_r), keep, between)
     pending += more
-    for copy in sent:
-        copy.wait_recv()
-    for n in range(32):
-        gram_ref[2 * n] = sums[n, 0]
-        gram_ref[2 * n + 1] = sums[n, 1]
+    eliminate(work, 8)
+    right_side[0:WIDTH, 0:CHUNK] = power[...]
+    right_side[WIDTH:] = jnp.zeros((384 - WIDTH, 2 * CHUNK), F32)
     for piece in range(NSUB):
         before(piece)
+    out = dot(work[0:WIDTH, 384:], right_side[...], (1, 0), HIGHEST)
+    basis_ref[...] = out[:, :CHUNK]
+    projected_ref[...] = out[:, CHUNK:]
     for copy in pending:
         copy.wait_send()
 
@@ -458,26 +469,31 @@
     return jnp.concatenate(R, 0)
 
 
-def basis_kernel(gram_ref, power_ref, second_ref, basis_ref, projected_ref, work):
-    work[WIDTH:] = jnp.zeros((384 - WIDTH, 640), F32)
+def unpack_gram(sums, work):
+    work[...] = jnp.zeros_like(work)
     for n, (g, t) in enumerate(packed_tiles()):
-        work[g * 8 : g * 8 + 8, t * CHUNK : (t + 1) * CHUNK] = gram_ref[n] * (1.0 / 32768.0)
+        work[g * 8 : g * 8 + 8, t * CHUNK : (t + 1) * CHUNK] = sums[n // 2, n % 2] * (1.0 / 32768.0)
     work[0:128, 128:256] = work[128:256, 0:128].T
     work[0:128, 256:384] = work[256:384, 0:128].T
     work[128:256, 256:384] = work[256:384, 128:256].T
-    work[0:WIDTH, 384:512] = power_ref[...]
-    work[0:WIDTH, 512:640] = second_ref[...]
-    for panel in range(9):
-        r0 = panel * 32
-        tile, off = r0 // CHUNK, r0 % CHUNK
-        right = invert_factor(work[r0 : r0 + 32, tile * CHUNK : (tile + 1) * CHUNK], off)
-        upper = dot(right, work[tile * CHUNK : (tile + 1) * CHUNK, tile * CHUNK :], (1, 0), HIGHEST)
-        if panel < 8:
-            below = work[r0 + 32 : WIDTH, tile * CHUNK : (tile + 1) * CHUNK]
-            lower = dot(below, right, (1, 1), HIGHEST)
-            work[r0 + 32 : WIDTH, tile * CHUNK :] -= dot(lower, upper, (1, 0), HIGHEST)
-        basis_ref[r0 : r0 + 32] = upper[:, -256:-128]
-        projected_ref[r0 : r0 + 32] = upper[:, -128:]
+    row = lax.broadcasted_iota(jnp.int32, (CHUNK, CHUNK), 0)
+    lane = lax.broadcasted_iota(jnp.int32, (CHUNK, CHUNK), 1)
+    one = (row == lane).astype(F32)
+    for t in range(3):
+        work[t * CHUNK : (t + 1) * CHUNK, 384 + t * CHUNK : 384 + (t + 1) * CHUNK] = one
+
+
+def eliminate(work, panel):
+    r0 = panel * 32
+    tile, off = r0 // CHUNK, r0 % CHUNK
+    block = slice(tile * CHUNK, (tile + 1) * CHUNK)
+    span = slice(tile * CHUNK, 384 + (tile + 1) * CHUNK)
+    right = invert_factor(work[r0 : r0 + 32, block], off)
+    upper = dot(right, work[block, span], (1, 0), HIGHEST)
+    if panel < 8:
+        lower = dot(work[r0 + 32 : WIDTH, block], right, (1, 1), HIGHEST)
+        work[r0 + 32 : WIDTH, span] -= dot(lower, upper, (1, 0), HIGHEST)
+    work[r0 : r0 + 32, 384 : 384 + (tile + 1) * CHUNK] = upper[:, 384 - tile * CHUNK :]
 
 
 def sem(*shape):
@@ -495,15 +511,11 @@
     hbm = pl.BlockSpec(memory_space=pl.ANY)
     smem = pl.BlockSpec(memory_space=pltpu.SMEM)
     V = pltpu.VMEM
-    power, second, gram = pl.pallas_call(
+    basis, projected = pl.pallas_call(
         sample_kernel,
-        out_shape=[
-            jax.ShapeDtypeStruct((WIDTH, CHUNK), F32),
-            jax.ShapeDtypeStruct((WIDTH, CHUNK), F32),
-            jax.ShapeDtypeStruct((PACKED, 8, CHUNK), F32),
-        ],
+        out_shape=[jax.ShapeDtypeStruct((WIDTH, CHUNK), F32)] * 2,
         in_specs=[hbm, smem, vmem],
-        out_specs=[vmem, vmem, vmem],
+        out_specs=[vmem, vmem],
         scratch_shapes=[
             V((SLOTS + 1, CHUNK, CHUNK), BF16),
             V((4096, 1024), BF16),
@@ -532,6 +544,9 @@
             V((32, 2, 8, CHUNK), F32),
             V((32, 2, 8, CHUNK), F32),
             V((NZ, 2, 8, CHUNK), F32),
+            V((WIDTH, CHUNK), F32),
+            V((384, 768), F32),
+            V((384, 2 * CHUNK), F32),
             *sem(NSUB, 7),
             *sem(NSUB, 7),
             *sem(NSUB, 7),
@@ -550,14 +565,6 @@
         ),
     )(blocks[0, 0], slots, sketch.T)
 
-    basis, projected = pl.pallas_call(
-        basis_kernel,
-        out_shape=[jax.ShapeDtypeStruct((WIDTH, CHUNK), F32)] * 2,
-        in_specs=[vmem] * 3,
-        out_specs=[vmem] * 2,
-        scratch_shapes=[V((384, 640), F32)],
-        compiler_params=pltpu.CompilerParams(vmem_limit_bytes=40 << 20),
-    )(gram, power, second)
     return (basis.T, projected.T)
 
 

time: 174 us -> 167 us (0.960)
  Pallas kernels: 169 us -> 161 us
    pallas_call x1 -> x0, Pallas kernels: 13.2 us -> none  [local(): pl.pallas_call(basis_kernel, out_shape=[jax.ShapeDtypeStruct((WIDTH, CHUN...]
    pallas_call x1, Pallas kernels: 156 us -> 161 us  [local(): pl.pallas_call(sample_kernel, out_shape=[jax.ShapeDtypeStruct((WIDTH, CHU...]
where the time goes in v3:
time: 167 us
  Pallas kernels  161 us (96%)
  local copies, waits for them, and re-layouts  3.16 us (2%)
    pallas_call x1, Pallas kernels, local(): pl.pallas_call(sample_kernel, out_shape=[jax.ShapeDtypeStruct((WIDTH, CHU...  161 us

profile of v3, /device:TPU:1, one launch (start us, length us, event | category | flops | bytes accessed | tf_op | source)
XLA Modules:
  0.0 166.5 jit_solution(5678897249830079552)
XLA Ops:
  1.3 0.7 compare_select_fusion
  1.9 0.7 select_reduce_fusion.slot_ref
  2.6 160.7 %shard_map.59 = (f32[288,128]{1,0:T(8,128)}, f32[288,128]{1,0:T(8,128)}) custom-call(bf16[96,128,128]{2,1,0:T(8,128)(2,1)} %bitcast.8, s32[256]{0:T(256)} %select_reduce_fusion.slot_ref, bf16[288,128]{1,0:T(8,128)(2,1)} %bitcast.11), custom_call_target="tpu_custom_call" | custom-call | tf_op jit(solution)/shard_map/pallas_call | solution.py:514
  163.3 1.6 copy.9
  164.9 1.6 copy.10

commit v4 on v3

--- a/solution.py
+++ b/solution.py
@@ -168,41 +168,47 @@
         compute(me.k, y)
     pending.extend(crossing)
     low, high = pl.ds(0, HALF), pl.ds(HALF, HALF)
-    first = []
+    first, along_x = [], []
     for i, y in enumerate(order):
         crossing[i].wait_recv()
         for x in range(SIDE):
             summed[y, x] = (part[me.k, y, x] + other[y, x]).astype(summed.dtype)
+        group = []
+        for j in (2, 1, 3):
+            n = 7 + 3 * i + j
+            x = (me.x + j) % SIDE
+            group.append(
+                send(summed.at[y, x, low], inbox.at[0, j - 1, i], send_sem.at[n], recv_sem.at[n], me.x_peer(j))
+            )
+        along_x.append(group)
         if i < 3:
             n = 4 + i
             first.append(
                 send(summed.at[y, :, high], inbox.at[1, i], send_sem.at[n], recv_sem.at[n], me.y_peer(i + 1))
             )
-    for i in range(3):
-        n = 7 + i
-        x = (me.x + i + 1) % SIDE
-        first.append(send(summed.at[:, x, low], inbox.at[0, i], send_sem.at[n], recv_sem.at[n], me.x_peer(i + 1)))
+    second = []
+    for i, y in enumerate(order):
+        for copy in along_x[i]:
+            copy.wait_recv()
+        pending.extend(along_x[i])
+        total = summed[y, me.x, low].astype(F32)
+        for j in range(3):
+            total += inbox[0, j, i].astype(F32)
+        totals[0, y] = total.astype(totals.dtype)
+        if i < 3:
+            n = 20 + i
+            second.append(send(totals.at[0, y], inbox2.at[0, i], send_sem.at[n], recv_sem.at[n], me.y_peer(i + 1)))
     for copy in first:
         copy.wait_recv()
     pending.extend(first)
-    second = []
-    for i in (1, 2, 3, 0):
-        y, x = (me.y + i) % SIDE, (me.x + i) % SIDE
-        total = summed[y, me.x, low].astype(F32)
-        for j in range(3):
-            total += inbox[0, j, y].astype(F32)
-        totals[0, y] = total.astype(totals.dtype)
-        if i:
-            n = 9 + i
-            second.append(
-                send(totals.at[0, y], inbox2.at[0, i - 1], send_sem.at[n], recv_sem.at[n], me.y_peer(i))
-            )
+    for i in (2, 1, 3, 0):
+        x = (me.x + i) % SIDE
         total = summed[me.y, x, high].astype(F32)
         for j in range(3):
             total += inbox[1, j, x].astype(F32)
         totals[1, x] = total.astype(totals.dtype)
         if i:
-            n = 12 + i
+            n = 22 + i
             second.append(
                 send(totals.at[1, x], inbox2.at[1, i - 1], send_sem.at[n], recv_sem.at[n], me.x_peer(i))
             )
@@ -223,40 +229,40 @@
     pending = []
     k, y, x = me.k, me.y, me.x
     low, high = pl.ds(0, HALF), pl.ds(HALF, HALF)
-    first = []
+    own_low, own_high = full.at[k, y, x, low], full.at[k, y, x, high]
+    count = [0]
+
+    def start(block, peer):
+        n = count[0]
+        count[0] += 1
+        copy = send(block, block, send_sem.at[n], recv_sem.at[n], peer)
+        pending.append(copy)
+        return copy
+
+    first = [(start(own_low, me.y_peer(i)), start(own_high, me.x_peer(i))) for i in (1, 2, 3)]
+    second = {i: [start(own_low, me.x_peer(i)), start(own_high, me.y_peer(i))] for i in (1, 2, 3)}
+    third = [start(full.at[k, y, x], me.sibling())]
+    between[0]()
     for i in (1, 2, 3):
-        block = full.at[k, y, x, low]
-        first.append(send(block, block, send_sem.at[i - 1], recv_sem.at[i - 1], me.y_peer(i)))
-        block = full.at[k, y, x, high]
-        first.append(send(block, block, send_sem.at[i + 2], recv_sem.at[i + 2], me.x_peer(i)))
-    between[0]()
-    for copy in first:
-        copy.wait_recv()
-    pending.extend(first)
-    second = []
-    for i in (1, 2, 3):
-        block = full.at[k, :, x, low]
-        second.append(send(block, block, send_sem.at[i + 5], recv_sem.at[i + 5], me.x_peer(i)))
-        block = full.at[k, y, :, high]
-        second.append(send(block, block, send_sem.at[i + 8], recv_sem.at[i + 8], me.y_peer(i)))
-    third = []
-
-    def cross(n, block):
-        third.append(send(block, block, send_sem.at[n], recv_sem.at[n], me.sibling()))
-
-    cross(12, full.at[k, :, x, low])
-    cross(13, full.at[k, y, :, high])
+        first[i - 1][0].wait_recv()
+        block = full.at[k, (y - i + SIDE) % SIDE, x, low]
+        for j in (2, 1, 3):
+            second[j].append(start(block, me.x_peer(j)))
+        third.append(start(block, me.sibling()))
+        first[i - 1][1].wait_recv()
+        block = full.at[k, y, (x - i + SIDE) % SIDE, high]
+        for j in (2, 1, 3):
+            second[j].append(start(block, me.y_peer(j)))
+        third.append(start(block, me.sibling()))
     between[1]()
     for i in (1, 3, 2):
-        second[2 * i - 2].wait_recv()
-        cross(13 + i, full.at[k, :, (x - i + SIDE) % SIDE, low])
-        second[2 * i - 1].wait_recv()
-        cross(16 + i, full.at[k, (y - i + SIDE) % SIDE, :, high])
-    pending.extend(second)
+        for copy in second[i]:
+            copy.wait_recv()
+        third.append(start(full.at[k, :, (x - i + SIDE) % SIDE, low], me.sibling()))
+        third.append(start(full.at[k, (y - i + SIDE) % SIDE, :, high], me.sibling()))
     between[2]()
     for copy in third:
         copy.wait_recv()
-    pending.extend(third)
     return pending
 
 
@@ -275,21 +281,20 @@
     return compute
 
 
-def flatten(full, flat):
+def backward(full, flat, matrix, part, core, first):
+    start = pl.multiple_of(core * 2048, 2048)
+
+    def flatten(n, carry):
+        flat[:, pl.ds(pl.multiple_of(n * CHUNK, CHUNK), CHUNK)] = full[core, n // SIDE, n % SIDE]
+        return carry
+
+    lax.fori_loop(0, 16, flatten, 0)
+
     def body(n, carry):
-        core, y, x = n // 16, (n // 4) % 4, n % 4
-        flat[:, pl.ds(pl.multiple_of(n * CHUNK, CHUNK), CHUNK)] = full[core, y, x]
-        return carry
-
-    lax.fori_loop(0, 32, body, 0)
-
-
-def backward(flat, matrix, part):
-    def body(n, carry):
-        start = pl.multiple_of(n * 256, 256)
-        out = dot(flat[...], matrix[:, pl.ds(start, 256)], (1, 0))
-        part[2 * n] = out[:, :CHUNK]
-        part[2 * n + 1] = out[:, CHUNK:]
+        out = dot(flat[...], matrix[pl.ds(start, 2048), pl.ds(pl.multiple_of(n * 256, 256), 256)], (1, 0))
+        for half in range(2):
+            share = out[:, half * CHUNK : (half + 1) * CHUNK]
+            part[2 * n + half] = share if first else part[2 * n + half] + share
         return carry
 
     lax.fori_loop(0, 4, body, 0)
@@ -334,9 +339,9 @@
         copy.wait_send()
     full[me.k, me.y, me.x, pl.ds(0, HALF)] = halves[0].astype(BF16)
     full[me.k, me.y, me.x, pl.ds(HALF, HALF)] = halves[1].astype(BF16)
-    pending += gather_col(me, full, (fa_s, fa_r))
-    flatten(full, flat)
-    backward(flat, matrix, zpart)
+    hooks = (lambda: None, lambda: None, lambda: backward(full, flat, matrix, zpart, me.k, True))
+    pending += gather_col(me, full, (fa_s, fa_r), hooks)
+    backward(full, flat, matrix, zpart, 1 - me.k, False)
 
     def finish(piece, total):
         middle[pl.ds(piece * SUB, SUB), lanes(me.r)] = total.astype(BF16)
@@ -394,10 +399,13 @@
         for i in range(1, 32):
             sent.append(send(sums.at[me.c], sums.at[me.c], g3_s.at[i], g3_r.at[i], me.col_peer(i)))
 
-    pending += gather_col(me, full2, (fb_s, fb_r), (gram_part, gram_col, gram_row))
+    def gram_row_and_pass():
+        gram_row()
+        backward(full2, flat, matrix, zpart, me.k, True)
+
+    pending += gather_col(me, full2, (fb_s, fb_r), (gram_part, gram_col, gram_row_and_pass))
     pending.extend(sent)
-    flatten(full2, flat)
-    backward(flat, matrix, zpart)
+    backward(full2, flat, matrix, zpart, 1 - me.k, False)
 
     def keep(piece, total):
         right_side[piece * SUB : (piece + 1) * SUB, CHUNK:] = total
@@ -533,7 +541,7 @@
             V((2, SIDE, HALF, CHUNK), BF16),
             V((2, SIDE, SIDE, WIDTH, CHUNK), BF16),
             V((2, SIDE, SIDE, WIDTH, CHUNK), BF16),
-            V((WIDTH, 4096), BF16),
+            V((WIDTH, 2048), BF16),
             V((NZ, WIDTH, CHUNK), F32),
             V((4, WIDTH, CHUNK), F32),
             V((3, WIDTH, CHUNK), F32),
@@ -551,10 +559,10 @@
             *sem(NSUB, 7),
             *sem(NSUB, 7),
             *sem(NSUB, 7),
-            *sem(16),
-            *sem(16),
-            *sem(20),
-            *sem(20),
+            *sem(26),
+            *sem(26),
+            *sem(43),
+            *sem(43),
             *sem(32),
             *sem(8),
             *sem(32),

time: 167 us -> 164 us (0.982)
  Pallas kernels: 161 us -> 158 us
    pallas_call x1, Pallas kernels: 161 us -> 158 us  [local(): pl.pallas_call(sample_kernel, out_shape=[jax.ShapeDtypeStruct((WIDTH, CHU...]
where the time goes in v4:
time: 164 us
  Pallas kernels  158 us (96%)
  local copies, waits for them, and re-layouts  3.16 us (2%)
    pallas_call x1, Pallas kernels, local(): pl.pallas_call(sample_kernel, out_shape=[jax.ShapeDtypeStruct((WIDTH, CHU...  158 us

profile of v4, /device:TPU:1, one launch (start us, length us, event | category | flops | bytes accessed | tf_op | source)
XLA Modules:
  0.0 163.7 jit_solution(9365824252775209408)
XLA Ops:
  1.3 0.7 compare_select_fusion
  1.9 0.7 select_reduce_fusion.slot_ref
  2.6 157.9 %shard_map.59 = (f32[288,128]{1,0:T(8,128)}, f32[288,128]{1,0:T(8,128)}) custom-call(bf16[96,128,128]{2,1,0:T(8,128)(2,1)} %bitcast.8, s32[256]{0:T(256)} %select_reduce_fusion.slot_ref, bf16[288,128]{1,0:T(8,128)(2,1)} %bitcast.11), custom_call_target="tpu_custom_call" | custom-call | tf_op jit(solution)/shard_map/pallas_call | solution.py:522
  160.5 1.6 copy.9
  162.1 1.6 copy.10

commit v5 on v4

--- a/solution.py
+++ b/solution.py
@@ -102,8 +102,8 @@
             if step < 3:
                 copies.append(goes[piece](step, -1))
             held[piece] = copies
-        if step == 0 and meanwhile is not None:
-            meanwhile()
+        if meanwhile is not None:
+            meanwhile(step)
     for piece in range(NSUB):
         for copy in held[piece]:
             copy.wait_recv()
@@ -281,23 +281,26 @@
     return compute
 
 
-def backward(full, flat, matrix, part, core, first):
-    start = pl.multiple_of(core * 2048, 2048)
-
-    def flatten(n, carry):
+def flatten(full, flat, core):
+    def body(n, carry):
         flat[:, pl.ds(pl.multiple_of(n * CHUNK, CHUNK), CHUNK)] = full[core, n // SIDE, n % SIDE]
         return carry
 
-    lax.fori_loop(0, 16, flatten, 0)
-
-    def body(n, carry):
+    lax.fori_loop(0, 16, body, 0)
+
+
+def backward(me, flat, matrix, part, core, first, steps):
+    start = pl.multiple_of(core * 2048, 2048)
+
+    def body(step, carry):
+        n = (me.r // 2 + 6 - step) % 4
         out = dot(flat[...], matrix[pl.ds(start, 2048), pl.ds(pl.multiple_of(n * 256, 256), 256)], (1, 0))
         for half in range(2):
             share = out[:, half * CHUNK : (half + 1) * CHUNK]
             part[2 * n + half] = share if first else part[2 * n + half] + share
         return carry
 
-    lax.fori_loop(0, 4, body, 0)
+    lax.fori_loop(*steps, body, 0)
 
 
 def packed_tiles():
@@ -316,9 +319,12 @@
     pending = []
     load = pltpu.make_async_copy(blocks_ref, tiles.at[pl.ds(0, SLOTS)], local.at[0])
     load.start()
-    operand[:, lanes(me.r)] = sketch_ref[...]
+    own = pltpu.make_async_copy(sketch_ref, operand.at[:, lanes(me.r)], local.at[1])
+    own.start()
     tiles[SLOTS] = jnp.zeros((CHUNK, CHUNK), BF16)
     greet([me.col_peer(i) for i in range(1, 32)] + [me.z_peer(i) for i in range(1, NZ)])
+
+    own.wait()
 
     def build(n, carry):
         start = pl.multiple_of(((n % 2) * 16 + n // 2) * CHUNK, CHUNK)
@@ -326,11 +332,12 @@
             matrix[pl.ds(start, CHUNK), t * CHUNK : (t + 1) * CHUNK] = tiles[slot_ref[n * 8 + t]]
         return carry
 
-    def build_all():
-        load.wait()
-        lax.fori_loop(0, 32, build, 0)
-
-    pending += gather_z(me, operand, (ga_s, ga_r), lambda piece: None, build_all)
+    def build_some(step):
+        if step == 0:
+            load.wait()
+        lax.fori_loop(8 * step, 8 * step + 8, build, 0)
+
+    pending += gather_z(me, operand, (ga_s, ga_r), lambda piece: None, build_some)
 
     halves, more = scatter_col(
         me, part, other, sum_f, inbox_f, inbox2_f, totals_f, (ca_s, ca_r), forward(operand, matrix, part)
@@ -339,14 +346,26 @@
         copy.wait_send()
     full[me.k, me.y, me.x, pl.ds(0, HALF)] = halves[0].astype(BF16)
     full[me.k, me.y, me.x, pl.ds(HALF, HALF)] = halves[1].astype(BF16)
-    hooks = (lambda: None, lambda: None, lambda: backward(full, flat, matrix, zpart, me.k, True))
+    def own_half(rows):
+        flatten(rows, flat, me.k)
+        backward(me, flat, matrix, zpart, me.k, True, (0, 4))
+
+    def other_half(steps):
+        backward(me, flat, matrix, zpart, 1 - me.k, False, steps)
+
+    hooks = (lambda: None, lambda: None, lambda: own_half(full))
     pending += gather_col(me, full, (fa_s, fa_r), hooks)
-    backward(full, flat, matrix, zpart, 1 - me.k, False)
+    flatten(full, flat, 1 - me.k)
+    other_half((0, 2))
 
     def finish(piece, total):
         middle[pl.ds(piece * SUB, SUB), lanes(me.r)] = total.astype(BF16)
 
-    before, more = scatter_z(me, zpart, up, down, (za_s, za_r), finish)
+    def rest(step):
+        if step == 0:
+            other_half((2, 4))
+
+    before, more = scatter_z(me, zpart, up, down, (za_s, za_r), finish, rest)
     pending += gather_z(me, middle, (gb_s, gb_r), before)
     for copy in more:
         copy.wait_send()
@@ -401,17 +420,19 @@
 
     def gram_row_and_pass():
         gram_row()
-        backward(full2, flat, matrix, zpart, me.k, True)
+        own_half(full2)
 
     pending += gather_col(me, full2, (fb_s, fb_r), (gram_part, gram_col, gram_row_and_pass))
     pending.extend(sent)
-    backward(full2, flat, matrix, zpart, 1 - me.k, False)
+    flatten(full2, flat, 1 - me.k)
+    other_half((0, 2))
 
     def keep(piece, total):
         right_side[piece * SUB : (piece + 1) * SUB, CHUNK:] = total
 
     def between(step):
         if step == 0:
+            other_half((2, 4))
             for copy in sent:
                 copy.wait_recv()
             unpack_gram(sums, work)
@@ -497,11 +518,30 @@
     block = slice(tile * CHUNK, (tile + 1) * CHUNK)
     span = slice(tile * CHUNK, 384 + (tile + 1) * CHUNK)
     right = invert_factor(work[r0 : r0 + 32, block], off)
-    upper = dot(right, work[block, span], (1, 0), HIGHEST)
+    right_high, right_low = halves_of(right)
+    work_high, work_low = halves_of(work[block, span])
+    both = dot(jnp.concatenate([right_high, right_low], 0), work_high, (1, 0))
+    upper = both[:32] + both[32:] + dot(right_high, work_low, (1, 0))
     if panel < 8:
-        lower = dot(work[r0 + 32 : WIDTH, block], right, (1, 1), HIGHEST)
-        work[r0 + 32 : WIDTH, span] -= dot(lower, upper, (1, 0), HIGHEST)
+        none = jnp.zeros((32, CHUNK), BF16)
+        thrice_high = jnp.concatenate([right_high] * 3 + [none], 0)
+        thrice_low = jnp.concatenate([right_low] * 3 + [none], 0)
+        below_high, below_low = halves_of(work[r0 + 32 : WIDTH, block])
+        lower = dot(below_high, thrice_high, (1, 1)) + dot(below_high, thrice_low, (1, 1)) + dot(below_low, thrice_high, (1, 1))
+        lower_high, lower_low = halves_of(lower)
+        lane = lax.broadcasted_iota(jnp.int32, lower.shape, 1)
+        mixed = jnp.where(lane < 64, lower_high.astype(F32), lower_low.astype(F32)).astype(BF16)
+        upper_high, upper_low = halves_of(upper)
+        zero = jnp.zeros(upper.shape, BF16)
+        work[r0 + 32 : WIDTH, span] -= dot(
+            mixed, jnp.concatenate([upper_high, upper_low, upper_high, zero], 0), (1, 0)
+        )
     work[r0 : r0 + 32, 384 : 384 + (tile + 1) * CHUNK] = upper[:, 384 - tile * CHUNK :]
+
+
+def halves_of(value):
+    high = value.astype(BF16)
+    return high, (value - high.astype(F32)).astype(BF16)
 
 
 def sem(*shape):
@@ -516,13 +556,13 @@
     slots = jnp.min(jnp.where(hit, lax.iota(jnp.int32, SLOTS)[None, :], SLOTS), axis=1)
 
     vmem = pl.BlockSpec(memory_space=pltpu.VMEM)
-    hbm = pl.BlockSpec(memory_space=pl.ANY)
+    hbm = pl.BlockSpec(memory_space=pltpu.HBM)
     smem = pl.BlockSpec(memory_space=pltpu.SMEM)
     V = pltpu.VMEM
     basis, projected = pl.pallas_call(
         sample_kernel,
         out_shape=[jax.ShapeDtypeStruct((WIDTH, CHUNK), F32)] * 2,
-        in_specs=[hbm, smem, vmem],
+        in_specs=[hbm, smem, hbm],
         out_specs=[vmem, vmem],
         scratch_shapes=[
             V((SLOTS + 1, CHUNK, CHUNK), BF16),
@@ -566,10 +606,10 @@
             *sem(32),
             *sem(8),
             *sem(32),
-            DMA((1,)),
+            DMA((2,)),
         ],
         compiler_params=pltpu.CompilerParams(
-            collective_id=1, has_side_effects=True, vmem_limit_bytes=56 << 20
+            collective_id=1, has_side_effects=True, vmem_limit_bytes=52 << 20
         ),
     )(blocks[0, 0], slots, sketch.T)
 

time: 164 us -> 159 us (0.970)
  Pallas kernels: 158 us -> 154 us
    pallas_call x1, Pallas kernels: 158 us -> 154 us  [local(): pl.pallas_call(sample_kernel, out_shape=[jax.ShapeDtypeStruct((WIDTH, CHU...]
where the time goes in v5:
time: 159 us; the launch traced here: 158 us
  Pallas kernels  154 us (97%)
  local copies, waits for them, and re-layouts  2.2 us (1%)
    pallas_call x1, Pallas kernels, local(): pl.pallas_call(sample_kernel, out_shape=[jax.ShapeDtypeStruct((WIDTH, CHU...  154 us

profile of v5, /device:TPU:1, one launch (start us, length us, event | category | flops | bytes accessed | tf_op | source)
XLA Modules:
  0.0 158.2 jit_solution(1786198285062905691)
XLA Ops:
  1.3 0.7 compare_select_fusion
  1.9 0.1 select_reduce_fusion.slot_ref
  2.0 0.0 copy-start
  2.0 0.9 copy-done
  2.9 153.9 %shard_map.59 = (f32[288,128]{1,0:T(8,128)S(1)}, f32[288,128]{1,0:T(8,128)S(1)}) custom-call(bf16[96,128,128]{2,1,0:T(8,128)(2,1)} %bitcast.11, s32[256]{0:T(256)S(1)} %select_reduce_fusion.slot_ref, bf16[288,128]{1,0:T(8,128)(2,1)S(1)} %bitcast.10), custom_call_target="tpu_custom_call" | custom-call | tf_op jit(solution)/shard_map/pallas_call | solution.py:562
  156.9 0.7 copy.9
  157.5 0.7 copy.10
Async XLA Ops:
  2.0 0.9 copy-start

commit v6 on v5

--- a/solution.py
+++ b/solution.py
@@ -156,7 +156,7 @@
     return before, pending
 
 
-def scatter_col(me, part, other, summed, inbox, inbox2, totals, sems, compute):
+def scatter_col(me, part, other, summed, relay_x, relay_y, inbox, inbox2, totals, sems, compute):
     send_sem, recv_sem = sems
     pending = []
     order = [(me.y + i) % SIDE for i in (1, 2, 3, 0)]
@@ -168,53 +168,64 @@
         compute(me.k, y)
     pending.extend(crossing)
     low, high = pl.ds(0, HALF), pl.ds(HALF, HALF)
-    first, along_x = [], []
+    def start(n, src, dst, peer):
+        copy = send(src, dst, send_sem.at[n], recv_sem.at[n], peer)
+        pending.append(copy)
+        return copy
+
+    def add_to(ref, own):
+        ref[...] = (ref[...].astype(F32) + own.astype(F32)).astype(ref.dtype)
+
+    ways = (1, 3, 1, 3)
+    far_x, near_x = [], []
     for i, y in enumerate(order):
         crossing[i].wait_recv()
         for x in range(SIDE):
             summed[y, x] = (part[me.k, y, x] + other[y, x]).astype(summed.dtype)
-        group = []
-        for j in (2, 1, 3):
-            n = 7 + 3 * i + j
-            x = (me.x + j) % SIDE
-            group.append(
-                send(summed.at[y, x, low], inbox.at[0, j - 1, i], send_sem.at[n], recv_sem.at[n], me.x_peer(j))
-            )
-        along_x.append(group)
-        if i < 3:
-            n = 4 + i
-            first.append(
-                send(summed.at[y, :, high], inbox.at[1, i], send_sem.at[n], recv_sem.at[n], me.y_peer(i + 1))
+        far_x.append(start(7 + 3 * i, summed.at[y, (me.x + 2) % SIDE, low], relay_x.at[i], me.x_peer(ways[i])))
+        back = 4 - ways[i]
+        near_x.append(
+            start(8 + 3 * i, summed.at[y, (me.x + back) % SIDE, low], inbox.at[0, 1, i], me.x_peer(back))
+        )
+        if i == 0:
+            near_y = [start(4, summed.at[y, pl.ds(2, 2), high], inbox.at[1, 0, pl.ds(2, 2)], me.y_peer(1))]
+        if i == 1:
+            far_y = [
+                start(5, summed.at[y, pl.ds(0, 2), high], relay_y.at[0], me.y_peer(1)),
+                start(6, summed.at[y, pl.ds(2, 2), high], relay_y.at[1], me.y_peer(3)),
+            ]
+        if i == 2:
+            near_y.append(start(26, summed.at[y, pl.ds(0, 2), high], inbox.at[1, 1, pl.ds(0, 2)], me.y_peer(3)))
+    passed_x, passed_y = [], []
+    for i, y in enumerate(order):
+        far_x[i].wait_recv()
+        add_to(relay_x.at[i], summed[y, (me.x + ways[i]) % SIDE, low])
+        passed_x.append(start(9 + 3 * i, relay_x.at[i], inbox.at[0, 0, i], me.x_peer(ways[i])))
+        if i in (1, 2):
+            h = i - 1
+            far_y[h].wait_recv()
+            add_to(relay_y.at[h], summed[(me.y + ways[h]) % SIDE, pl.ds(2 * h, 2), high])
+            passed_y.append(
+                start(27 + h, relay_y.at[h], inbox.at[1, h, pl.ds(2 * h, 2)], me.y_peer(ways[h]))
             )
     second = []
     for i, y in enumerate(order):
-        for copy in along_x[i]:
-            copy.wait_recv()
-        pending.extend(along_x[i])
-        total = summed[y, me.x, low].astype(F32)
-        for j in range(3):
-            total += inbox[0, j, i].astype(F32)
+        near_x[i].wait_recv()
+        passed_x[i].wait_recv()
+        total = summed[y, me.x, low].astype(F32) + inbox[0, 0, i].astype(F32) + inbox[0, 1, i].astype(F32)
         totals[0, y] = total.astype(totals.dtype)
         if i < 3:
-            n = 20 + i
-            second.append(send(totals.at[0, y], inbox2.at[0, i], send_sem.at[n], recv_sem.at[n], me.y_peer(i + 1)))
-    for copy in first:
+            second.append(start(20 + i, totals.at[0, y], inbox2.at[0, i], me.y_peer(i + 1)))
+    for copy in near_y + passed_y:
         copy.wait_recv()
-    pending.extend(first)
     for i in (2, 1, 3, 0):
         x = (me.x + i) % SIDE
-        total = summed[me.y, x, high].astype(F32)
-        for j in range(3):
-            total += inbox[1, j, x].astype(F32)
+        total = summed[me.y, x, high].astype(F32) + inbox[1, 0, x].astype(F32) + inbox[1, 1, x].astype(F32)
         totals[1, x] = total.astype(totals.dtype)
         if i:
-            n = 22 + i
-            second.append(
-                send(totals.at[1, x], inbox2.at[1, i - 1], send_sem.at[n], recv_sem.at[n], me.x_peer(i))
-            )
+            second.append(start(22 + i, totals.at[1, x], inbox2.at[1, i - 1], me.x_peer(i)))
     for copy in second:
         copy.wait_recv()
-    pending.extend(second)
     halves = []
     for h, mine in enumerate((me.y, me.x)):
         total = totals[h, mine].astype(F32)
@@ -239,17 +250,17 @@
         pending.append(copy)
         return copy
 
-    first = [(start(own_low, me.y_peer(i)), start(own_high, me.x_peer(i))) for i in (1, 2, 3)]
+    first = {i: (start(own_low, me.y_peer(i)), start(own_high, me.x_peer(i))) for i in (1, 3, 2)}
     second = {i: [start(own_low, me.x_peer(i)), start(own_high, me.y_peer(i))] for i in (1, 2, 3)}
     third = [start(full.at[k, y, x], me.sibling())]
     between[0]()
-    for i in (1, 2, 3):
-        first[i - 1][0].wait_recv()
+    for i in (1, 3, 2):
+        first[i][0].wait_recv()
         block = full.at[k, (y - i + SIDE) % SIDE, x, low]
         for j in (2, 1, 3):
             second[j].append(start(block, me.x_peer(j)))
         third.append(start(block, me.sibling()))
-        first[i - 1][1].wait_recv()
+        first[i][1].wait_recv()
         block = full.at[k, y, (x - i + SIDE) % SIDE, high]
         for j in (2, 1, 3):
             second[j].append(start(block, me.y_peer(j)))
@@ -309,14 +320,20 @@
 
 def sample_kernel(
     blocks_ref, slot_ref, sketch_ref, basis_ref, projected_ref,
-    tiles, matrix, operand, middle, part, other, sum_f, inbox_f, inbox2_f, totals_f,
-    sum_h, inbox_h, inbox2_h, totals_h, full, full2, flat, zpart, up, down, up2, down2, gram, packed, gathered, sums, sums_z,
+    tiles, matrix, operand, middle, part, other, sum_f, relay_x_f, relay_y_f, inbox_f, inbox2_f, totals_f,
+    sum_h, relay_x_h, relay_y_h, inbox_h, inbox2_h, totals_h, full, full2, flat, zpart, up, down, up2, down2, gram, packed, gathered, sums, sums_z,
     power, work, right_side,
     ga_s, ga_r, gb_s, gb_r, za_s, za_r, zb_s, zb_r, ca_s, ca_r, cb_s, cb_r, fa_s, fa_r, fb_s, fb_r,
     g1_s, g1_r, g2_s, g2_r, g3_s, g3_r, local,
 ):
     me = Place()
     pending = []
+
+    def drain():
+        for copy in pending:
+            copy.wait_send()
+        pending.clear()
+
     load = pltpu.make_async_copy(blocks_ref, tiles.at[pl.ds(0, SLOTS)], local.at[0])
     load.start()
     own = pltpu.make_async_copy(sketch_ref, operand.at[:, lanes(me.r)], local.at[1])
@@ -340,10 +357,9 @@
     pending += gather_z(me, operand, (ga_s, ga_r), lambda piece: None, build_some)
 
     halves, more = scatter_col(
-        me, part, other, sum_f, inbox_f, inbox2_f, totals_f, (ca_s, ca_r), forward(operand, matrix, part)
+        me, part, other, sum_f, relay_x_f, relay_y_f, inbox_f, inbox2_f, totals_f, (ca_s, ca_r), forward(operand, matrix, part)
     )
-    for copy in more:
-        copy.wait_send()
+    pending += more
     full[me.k, me.y, me.x, pl.ds(0, HALF)] = halves[0].astype(BF16)
     full[me.k, me.y, me.x, pl.ds(HALF, HALF)] = halves[1].astype(BF16)
     def own_half(rows):
@@ -353,7 +369,7 @@
     def other_half(steps):
         backward(me, flat, matrix, zpart, 1 - me.k, False, steps)
 
-    hooks = (lambda: None, lambda: None, lambda: own_half(full))
+    hooks = (drain, lambda: None, lambda: own_half(full))
     pending += gather_col(me, full, (fa_s, fa_r), hooks)
     flatten(full, flat, 1 - me.k)
     other_half((0, 2))
@@ -364,14 +380,14 @@
     def rest(step):
         if step == 0:
             other_half((2, 4))
+            drain()
 
     before, more = scatter_z(me, zpart, up, down, (za_s, za_r), finish, rest)
     pending += gather_z(me, middle, (gb_s, gb_r), before)
-    for copy in more:
-        copy.wait_send()
+    pending += more
 
     halves, more = scatter_col(
-        me, part, other, sum_h, inbox_h, inbox2_h, totals_h, (cb_s, cb_r), forward(middle, matrix, part)
+        me, part, other, sum_h, relay_x_h, relay_y_h, inbox_h, inbox2_h, totals_h, (cb_s, cb_r), forward(middle, matrix, part)
     )
     pending += more
     power[pl.ds(0, HALF)] = halves[0]
@@ -392,6 +408,7 @@
             sent.append(
                 send(packed.at[pl.ds(2 * ((me.c + i) % 32), 2)], gathered.at[me.c], g1_s.at[i], g1_r.at[i], me.col_peer(i))
             )
+        drain()
 
     def gram_col():
         for copy in sent:
@@ -438,6 +455,8 @@
             unpack_gram(sums, work)
         for panel in (2 * step, 2 * step + 1):
             eliminate(work, panel)
+        if step == 2:
+            drain()
 
     before, more = scatter_z(me, zpart, up2, down2, (zb_s, zb_r), keep, between)
     pending += more
@@ -446,11 +465,10 @@
     right_side[WIDTH:] = jnp.zeros((384 - WIDTH, 2 * CHUNK), F32)
     for piece in range(NSUB):
         before(piece)
+    drain()
     out = dot(work[0:WIDTH, 384:], right_side[...], (1, 0), HIGHEST)
     basis_ref[...] = out[:, :CHUNK]
     projected_ref[...] = out[:, CHUNK:]
-    for copy in pending:
-        copy.wait_send()
 
 
 def over_lanes(block, lane):
@@ -550,10 +568,9 @@
 
 def local(blocks, positions, counts, sketch):
     places = positions[0, 0]
-    used = lax.iota(jnp.int32, SLOTS) < counts[0, 0]
-    where = jnp.where(used, places, -1)
-    hit = where[None, :] == lax.iota(jnp.int32, 256)[:, None]
-    slots = jnp.min(jnp.where(hit, lax.iota(jnp.int32, SLOTS)[None, :], SLOTS), axis=1)
+    number = lax.broadcasted_iota(jnp.int32, (256, SLOTS), 1)
+    hit = places[None, :] == lax.broadcasted_iota(jnp.int32, (256, SLOTS), 0)
+    slots = jnp.min(jnp.where(hit & (number < counts[0, 0]), number, SLOTS), axis=1)
 
     vmem = pl.BlockSpec(memory_space=pltpu.VMEM)
     hbm = pl.BlockSpec(memory_space=pltpu.HBM)
@@ -572,11 +589,15 @@
             V((2, SIDE, SIDE, WIDTH, CHUNK), F32),
             V((SIDE, SIDE, WIDTH, CHUNK), F32),
             V((SIDE, SIDE, WIDTH, CHUNK), F32),
-            V((2, 3, SIDE, HALF, CHUNK), F32),
+            V((SIDE, HALF, CHUNK), F32),
+            V((2, 2, HALF, CHUNK), F32),
+            V((2, 2, SIDE, HALF, CHUNK), F32),
             V((2, 3, HALF, CHUNK), F32),
             V((2, SIDE, HALF, CHUNK), F32),
             V((SIDE, SIDE, WIDTH, CHUNK), BF16),
-            V((2, 3, SIDE, HALF, CHUNK), BF16),
+            V((SIDE, HALF, CHUNK), BF16),
+            V((2, 2, HALF, CHUNK), BF16),
+            V((2, 2, SIDE, HALF, CHUNK), BF16),
             V((2, 3, HALF, CHUNK), BF16),
             V((2, SIDE, HALF, CHUNK), BF16),
             V((2, SIDE, SIDE, WIDTH, CHUNK), BF16),
@@ -599,8 +620,8 @@
             *sem(NSUB, 7),
             *sem(NSUB, 7),
             *sem(NSUB, 7),
-            *sem(26),
-            *sem(26),
+            *sem(29),
+            *sem(29),
             *sem(43),
             *sem(43),
             *sem(32),

time: 159 us -> 156 us (0.981)
  Pallas kernels: 154 us -> 151 us
    pallas_call x1, Pallas kernels: 154 us -> 151 us  [local(): pl.pallas_call(sample_kernel, out_shape=[jax.ShapeDtypeStruct((WIDTH, CHU...]
where the time goes in v6:
time: 156 us; the launch traced here: 155 us
  Pallas kernels  151 us (97%)
  local copies, waits for them, and re-layouts  2.2 us (1%)
    pallas_call x1, Pallas kernels, local(): pl.pallas_call(sample_kernel, out_shape=[jax.ShapeDtypeStruct((WIDTH, CHU...  151 us

profile of v6, /device:TPU:1, one launch (start us, length us, event | category | flops | bytes accessed | tf_op | source)
XLA Modules:
  0.0 155.4 jit_solution(3472513382552293365)
XLA Ops:
  1.3 0.8 select_reduce_fusion.slot_ref
  2.1 0.0 copy-start
  2.1 0.9 copy-done
  2.9 151.1 %shard_map.59 = (f32[288,128]{1,0:T(8,128)S(1)}, f32[288,128]{1,0:T(8,128)S(1)}) custom-call(bf16[96,128,128]{2,1,0:T(8,128)(2,1)} %bitcast.10, s32[256]{0:T(256)S(1)} %select_reduce_fusion.slot_ref, bf16[288,128]{1,0:T(8,128)(2,1)S(1)} %bitcast.9), custom_call_target="tpu_custom_call" | custom-call | tf_op jit(solution)/shard_map/pallas_call | solution.py:579
  154.1 0.7 copy.9
  154.7 0.7 copy.10
  (1 shorter events, 0.0 us)
Async XLA Ops:
  2.1 0.9 copy-start
